TPU v7x, 32 devices: a whole 2x2x4 slice. The times are simulated.
32 devices in a mesh: leaf: 8 (over y, x, core), probe: 4 (over z).
Axes of the slice: x: 2, y: 2, z: 4, core: 2. Of those that a mesh axis runs over, the one named last changes fastest.
Arguments:
- child_updates: bfloat16 [256, 512, 512], P('leaf'), may hold values from -0.25 to 0.25
- child_probes: bfloat16 [256, 131072], P('probe', 'leaf'), may hold values from -6 to 6
- child_dest: int32 [1024, 1], P('leaf'), may hold values from 0 to 7; in each aligned block of 128 rows (0 to 127, 128 to 255, ...) at most 32 rows name the same one
- child_rows: int32 [1024, 128], P('leaf'), may hold values from 0 to 2047
- parent_blocks: bfloat16 [512, 128, 128], P('leaf'), may hold values from -0.5 to 0.5
- coupling: int32 [512, 2], P('leaf'), may hold values from 0 to 15
- parent_probes: bfloat16 [256, 16384], P('probe', 'leaf'), may hold values from -6 to 6
- sketch: float32 [256, 128], P('probe'), may hold values from -0.375 to 0.375
- rank_one: int32 [8], P('leaf'), may hold values from 96 to 128, as said below
- rank_two: int32 [4], replicated, may hold values from 96 to 128, as said below
- rank_three: int32 [2], replicated, may hold values from 96 to 128, as said below
Outputs:
- basis_one: float32 [16384, 128], P(('leaf', 'probe'))
- basis_two: float32 [1024, 128], P('leaf')
- basis_three: float32 [1024, 128], P('leaf')
- top_sample: float32 [256, 1024], P('probe', 'leaf')
Inputs may be any that keep to these rules, and one draw needn't show every extreme that they name: `child_dest`: among the row blocks of one front group, no parent front is named by more than 32 blocks, and some parent front is named by exactly 32. `rank_one`: one node has rank 128. `rank_two`: one node has rank 128. `rank_three`: one node has rank 128.
All inputs are finite; a program needn't handle non-finite values.
Results may differ from a plain program's by a relative error of at most 0.0065.
Values may be sent and summed in bfloat16 or wider, within the bound.
A program may use at most 192 MiB of HBM per device.

v0:
```python
import jax
import jax.numpy as jnp
from jax import lax
from jax.sharding import PartitionSpec as P

highest = lax.Precision.HIGHEST


def partner_2(block, axis, stride):
    count = lax.axis_size(axis)
    route = []
    for low in range(count):
        high = low | 1 << stride
        if high != low and high < count:
            route += [(low, high), (high, low)]
    return lax.ppermute(block, axis, route)


def basis_from_gram(sketched, gram_matrix, rank_limit):
    factor = jnp.linalg.cholesky(gram_matrix)
    orthonormal = lax.linalg.triangular_solve(
        factor, sketched, left_side=False, lower=True, transpose_a=True
    )
    columns = jnp.arange(sketched.shape[1], dtype=jnp.int32)
    return jnp.where(columns[None, :] < rank_limit, orthonormal, jnp.zeros_like(orthonormal))


def chol_basis(sketched, rank_limit):
    gram_matrix = jnp.einsum("ra,rb->ab", sketched, sketched, precision=highest)
    return basis_from_gram(sketched, gram_matrix, rank_limit)


def on_device(
    child_updates,
    child_probes,
    child_dest,
    child_rows,
    parent_blocks,
    coupling,
    parent_probes,
    sketch,
    rank_one,
    rank_two,
    rank_three,
):
    leaf_count = lax.axis_size("leaf")
    probe_count = lax.axis_size("probe")
    leaf_index = lax.axis_index("leaf")
    probe_index = lax.axis_index("probe")
    local_probes = child_probes.shape[0]
    kid_count = child_updates.shape[0]
    kid_order = child_updates.shape[1]
    block_rows = child_rows.shape[1]
    block_count = child_rows.shape[0]
    front_rows = parent_probes.shape[1]
    rank_width = sketch.shape[1]
    updates = child_updates.reshape(kid_count, kid_order // block_rows, block_rows, kid_order)
    probe_cut = child_probes.reshape(local_probes, kid_count, kid_order)
    sampled = jnp.einsum("pck,cbik->cbpi", probe_cut, updates, preferred_element_type=jnp.float32)
    sampled = sampled.astype(jnp.bfloat16).reshape(block_count, local_probes, block_rows)
    targets = child_dest[:, 0]
    global_rows = (targets[:, None] * front_rows + child_rows).reshape(-1)
    values = jnp.moveaxis(sampled, 1, 0).reshape(local_probes, -1).astype(jnp.float32)
    partial_all = (
        jnp.zeros((local_probes, leaf_count * front_rows), jnp.float32)
        .at[:, global_rows]
        .add(values)
    )
    extended = lax.psum_scatter(partial_all, "leaf", scatter_dimension=1, tiled=True)
    pieces = parent_probes.reshape(local_probes, front_rows // block_rows, block_rows)
    picked = jnp.take(pieces, coupling[:, 1], axis=1)
    product = jnp.einsum("eik,pek->pei", parent_blocks, picked, preferred_element_type=jnp.float32)
    initial = (
        jnp.zeros(pieces.shape, jnp.float32)
        .at[:, coupling[:, 0]]
        .add(product)
        .reshape(local_probes, front_rows)
    )
    sample = initial + extended
    partial_sketch = jnp.einsum("pr,ps->rs", sample, sketch, precision=highest)
    share_rows = front_rows // probe_count
    sketched = lax.psum(partial_sketch, "probe")
    basis_front = chol_basis(sketched, rank_one[0])
    own_basis = lax.dynamic_slice_in_dim(basis_front, probe_index * share_rows, share_rows, 0)
    passed_one = jnp.dot(sample, basis_front, precision=highest)
    pair_bit = leaf_index % 2
    partner = partner_2(passed_one, "leaf", 0)
    stacked_two = jnp.where(
        pair_bit == 0,
        jnp.concatenate([passed_one, partner], 1),
        jnp.concatenate([partner, passed_one], 1),
    )
    sketched_two = lax.psum(
        jnp.einsum("pr,ps->rs", stacked_two, sketch, precision=highest), "probe"
    )
    merged_two = chol_basis(sketched_two, rank_two[leaf_index // 2])
    passed_two = jnp.dot(stacked_two, merged_two, precision=highest)
    quad_bit = leaf_index // 2 % 2
    partner_two = partner_2(passed_two, "leaf", 1)
    stacked_three = jnp.where(
        quad_bit == 0,
        jnp.concatenate([passed_two, partner_two], 1),
        jnp.concatenate([partner_two, passed_two], 1),
    )
    sketched_three = lax.psum(
        jnp.einsum("pr,ps->rs", stacked_three, sketch, precision=highest), "probe"
    )
    merged_three = chol_basis(sketched_three, rank_three[leaf_index // 4])
    passed_three = jnp.dot(stacked_three, merged_three, precision=highest)
    basis_two = lax.dynamic_slice_in_dim(merged_two, pair_bit * rank_width, rank_width, 0)
    basis_three = lax.dynamic_slice_in_dim(merged_three, quad_bit * rank_width, rank_width, 0)
    return (own_basis, basis_two, basis_three, passed_three)


def solution(mesh):
    return jax.shard_map(
        on_device,
        mesh=mesh,
        in_specs=(
            P("leaf", None, None),
            P("probe", "leaf"),
            P("leaf", None),
            P("leaf", None),
            P("leaf", None, None),
            P("leaf", None),
            P("probe", "leaf"),
            P("probe", None),
            P("leaf"),
            P(),
            P(),
        ),
        out_specs=(
            P(("leaf", "probe"), None),
            P("leaf", None),
            P("leaf", None),
            P("probe", "leaf"),
        ),
        check_vma=False,
    )
```

profile of v0, /device:TPU:0, one launch (start us, length us, event | category | flops | bytes accessed | tf_op | source)
XLA Modules:
  0.0 415.5 jit_solution(287475462165258878)
XLA Ops:
  7.2 0.0 reduce-scatter.2.cloned.1.call-start
  7.2 0.8 multiply_bitcast_fusion
  8.0 0.9 broadcast_add_fusion
  8.9 0.1 compare_select_fusion
  9.0 2.4 copy.47
  11.4 10.4 %convert_convert_fusion = f32[32,4,128,64]{2,3,1,0:T(8,128)} fusion(bf16[32,4,128,512]{3,2,1,0:T(8,128)(2,1)} %bitcast.91, bf16[64,32,512,1]{2,1,0,3:T(8,128)(2,1)S(1)} %bitcast.93), kind=kOutput, calls=%fused_computation.8 | convolution fusion | flops 1075838976 | bytes 23068672 | tf_op jit(solution)/shard_map/pck,cbik->cbpi/dot_general | solution.py:59
  21.8 6.9 %copy.34 = f32[64,128,128]{0,2,1:T(8,128)} copy(f32[64,128,128]{2,0,1:T(8,128)} %bitcast.92) | data formatting | bytes 8388608 | tf_op jit(solution)/shard_map/convert_element_type | solution.py:63
  28.7 91.3 %scatter_custom_fusion.1 = f32[64,16384]{0,1:T(8,128)} fusion(s32[16384]{0:T(1024)S(1)} %bitcast.97, f32[16384,64]{1,0:T(8,128)} %bitcast.94, f32[]{:T(128)} %constant.100.clone.1), kind=kCustom, calls=%fused_computation.3 | custom fusion | flops 1048576 | bytes 4194816 | tf_op jit(solution)/shard_map/scatter-add | solution.py:67
  120.0 0.0 reduce-scatter.2.cloned.1.call-update
  120.1 0.0 all-reduce.4.cloned.1.call-start
  120.1 0.6 copy-done.4
  120.7 0.3 copy-done.3
  121.0 0.1 copy_bitcast_fusion
  121.1 0.8 gather_fusion
  121.8 2.9 fusion.8
  124.8 7.1 %scatter_fusion = f32[64,16,128]{2,0,1:T(8,128)S(1)} fusion(f32[64,16,128]{2,0,1:T(8,128)S(1)} %broadcast_in_dim.47, s32[64]{0:T(128)S(1)} %get-tuple-element.19, f32[64,64,128]{2,1,0:T(8,128)} %fusion.8), kind=kCustom, calls=%fused_computation.1 | custom fusion | flops 524288 | bytes 6291712 | tf_op jit(solution)/shard_map/scatter-add | solution.py:76
  132.0 1.4 copy.42
  133.4 60.8 %reduce-scatter.2.cloned.1.call-done = f32[64,2048]{0,1:T(8,128)} async-done(((f32[64,16384]{0,1:T(8,128)}), f32[64,2048]{0,1:T(8,128)}) %reduce-scatter.2.cloned.1.call-update) | async-done | bytes 524304 | tf_op jit(solution)/shard_map/reduce_scatter | solution.py:69
  194.2 1.6 bitcast_add_fusion
  195.8 2.0 fusion.37
  197.8 0.0 all-reduce.4.cloned.1.call-update
  197.9 0.2 all-reduce.6.cloned.1.call-start
  198.8 51.1 %all-reduce.4.cloned.1.call-done = f32[2048,128]{1,0:T(8,128)} async-done(((f32[2048,128]{1,0:T(8,128)}), f32[2048,128]{1,0:T(8,128)}) %all-reduce.4.cloned.1.call-update) | async-done | bytes 1048592 | tf_op jit(solution)/shard_map/psum | solution.py:82
  249.8 3.4 fusion.38
  253.2 0.1 copy.36
  253.3 11.7 %cholesky.59 = f32[128,128]{1,0:T(8,128)S(1)} custom-call(f32[128,128]{1,0:T(8,128)S(1)} %fusion.21), custom_call_target="Cholesky" | custom-call | tf_op jit(solution)/shard_map/jit(cholesky)/cholesky | solution.py:20
  265.0 0.6 compare_reduce_fusion.2
  265.7 0.7 fusion.13
  266.4 9.8 %custom-call.8 = f32[1,128,128]{1,2,0:T(8,128)S(1)} custom-call(f32[1,128,128]{2,1,0:T(8,128)S(1)} %fusion.13), custom_call_target="InvertDiagBlocksLowerTriangular" | custom-call | tf_op jit(solution)/shard_map/triangular_solve | solution.py:21
  276.2 2.2 convolution_select_fusion
  278.4 1.9 fusion.39
  280.3 0.1 collective-permute-start
  280.4 1.2 collective-permute-done
  281.5 1.0 fusion.25
  282.6 0.0 all-reduce.6.cloned.1.call-update
  282.6 0.3 all-reduce.8.cloned.1.call-start
  282.9 0.6 dynamic_slice.16
  283.5 0.6 dynamic_slice.18
  284.1 0.6 iota_compare_fusion.3
  284.8 31.9 %all-reduce.6.cloned.1.call-done = f32[256,128]{1,0:T(8,128)} async-done(((f32[256,128]{1,0:T(8,128)}), f32[256,128]{1,0:T(8,128)}) %all-reduce.6.cloned.1.call-update) | async-done | bytes 131088 | tf_op jit(solution)/shard_map/psum | solution.py:93
  316.6 1.4 fusion.40
  318.0 0.1 copy.37
  318.1 11.7 %cholesky.70 = f32[128,128]{1,0:T(8,128)S(1)} custom-call(f32[128,128]{1,0:T(8,128)S(1)} %fusion.19), custom_call_target="Cholesky" | custom-call | tf_op jit(solution)/shard_map/jit(cholesky)/cholesky | solution.py:20
  329.8 0.6 compare_reduce_fusion.1
  330.5 0.7 fusion.14
  331.1 9.8 %custom-call.10 = f32[1,128,128]{1,2,0:T(8,128)S(1)} custom-call(f32[1,128,128]{2,1,0:T(8,128)S(1)} %fusion.14), custom_call_target="InvertDiagBlocksLowerTriangular" | custom-call | tf_op jit(solution)/shard_map/triangular_solve/custom-call.2 | solution.py:21
  341.0 1.2 fusion.6
  342.2 0.3 fusion.24
  342.4 1.5 collective-permute-start.1
  343.9 0.6 iota_compare_fusion.2
  344.6 1.8 collective-permute-done.1
  346.4 1.0 fusion.23
  347.5 1.7 constant_dynamic-slice_fusion.2
  349.2 0.7 copy.39
  349.9 31.9 %all-reduce.8.cloned.1.call-done = f32[256,128]{1,0:T(8,128)} async-done(((f32[256,128]{1,0:T(8,128)}), f32[256,128]{1,0:T(8,128)}) %all-reduce.8.cloned.1.call-update) | async-done | bytes 131088 | tf_op jit(solution)/shard_map/psum | solution.py:105
  381.8 1.4 fusion.41
  383.1 0.1 copy.38
  383.2 11.7 %cholesky.81 = f32[128,128]{1,0:T(8,128)S(1)} custom-call(f32[128,128]{1,0:T(8,128)S(1)} %fusion.17), custom_call_target="Cholesky" | custom-call | tf_op jit(solution)/shard_map/jit(cholesky)/cholesky | solution.py:20
  395.0 0.6 compare_reduce_fusion
  395.6 0.7 fusion.15
  396.3 9.8 %custom-call.11 = f32[1,128,128]{1,2,0:T(8,128)S(1)} custom-call(f32[1,128,128]{2,1,0:T(8,128)S(1)} %fusion.15), custom_call_target="InvertDiagBlocksLowerTriangular" | custom-call | tf_op jit(solution)/shard_map/triangular_solve/custom-call.2 | solution.py:21
  406.1 1.2 fusion.7
  407.4 0.7 copy.40
  408.1 0.9 fusion.22
  (26 shorter events, 0.3 us)
Async XLA Ops:
  7.2 114.7 %copy-start = (bf16[64,128,128]{2,1,0:T(8,128)(2,1)S(1)}, bf16[64,128,128]{2,1,0:T(8,128)(2,1)}, u32[]{:S(2)}) copy-start(bf16[64,128,128]{2,1,0:T(8,128)(2,1)} %param.18) | copy-start | bytes 6291460
  7.2 187.0 %reduce-scatter.2.cloned.1.call-start = ((), (), s32[]{:S(2)}) async-start(), calls=%async_computation.1 | async-start | bytes 9437184 | tf_op jit(solution)/shard_map/reduce_scatter | solution.py:69
  120.0 0.7 copy-start.4
  120.0 1.0 copy-start.3
  120.1 129.8 %all-reduce.4.cloned.1.call-start = ((), (), s32[]{:S(2)}) async-start(), calls=%async_computation.2 | async-start | bytes 2097152 | tf_op jit(solution)/shard_map/psum | solution.py:82
  124.8 71.0 %copy-start.2 = (f32[64,128]{1,0:T(8,128)S(1)}, f32[64,128]{1,0:T(8,128)}, u32[]{:S(2)}) copy-start(f32[64,128]{1,0:T(8,128)} %param.21) | copy-start | bytes 98308
  197.8 85.1 %copy-start.5 = (s32[4]{0:T(128)S(1)}, s32[4]{0:T(128)}, u32[]{:S(2)}) copy-start(s32[4]{0:T(128)} %param.23) | copy-start | bytes 52
  197.8 85.7 %copy-start.6 = (s32[2]{0:T(128)S(1)}, s32[2]{0:T(128)}, u32[]{:S(2)}) copy-start(s32[2]{0:T(128)} %param.24) | copy-start | bytes 28
  197.9 118.7 %all-reduce.6.cloned.1.call-start = ((), (), s32[]{:S(2)}) async-start(), calls=%async_computation.3 | async-start | bytes 262144 | tf_op jit(solution)/shard_map/psum | solution.py:93
  278.4 1.9 copy-start.1
  280.3 1.3 collective-permute-start
  282.6 99.2 %all-reduce.8.cloned.1.call-start = ((), (), s32[]{:S(2)}) async-start(), calls=%async_computation.4 | async-start | bytes 262144 | tf_op jit(solution)/shard_map/psum | solution.py:105
  342.4 4.0 collective-permute-start.1
Sparse Core Ops, SparseCore 0:
  120.2 73.9 reduce-scatter.1
  198.0 51.7 all-reduce.3
  282.7 33.8 all-reduce.5
  347.6 34.1 all-reduce.7
where the time goes:
time: 416 us
  waiting for transfers between devices  179 us (43%)
  other arithmetic  172 us (41%)
  matrix products  31.2 us (8%)
  local copies, waits for them, and re-layouts  17 us (4%)
  between operations  14.8 us (4%)
    scatter-add x1, other arithmetic, on_device(): partial_all = jnp.zeros((local_probes, leaf_count * front_rows), jnp.floa...  91.3 us
    reduce_scatter x1, waiting for transfers between devices, on_device(): lax.psum_scatter(partial_all, 'leaf', scatter_dimension=1, tiled=True)  60.8 us
    psum x1, waiting for transfers between devices, on_device(): sketched = lax.psum(partial_sketch, 'probe')  51.1 us
    another operation x9, other arithmetic, basis_from_gram(): factor = jnp.linalg.cholesky(gram_matrix)  37.2 us
    psum x1, waiting for transfers between devices, on_device(): lax.psum(jnp.einsum('pr,ps->rs', stacked_three, sketch, precision=highest...  31.9 us
    psum x1, waiting for transfers between devices, on_device(): lax.psum(jnp.einsum('pr,ps->rs', stacked_two, sketch, precision=highest),...  31.9 us
    another operation x6, other arithmetic, basis_from_gram(): lax.linalg.triangular_solve(factor, sketched, left_side=False, lower=True...  31.4 us
    dot_general x1, matrix products, on_device(): jnp.einsum('pck,cbik->cbpi', probe_cut, updates, preferred_element_type=j...  10.4 us
  transfers between devices with their start and end apart: 6, of which 6 were waited for; matrix products, arithmetic and copies ran while one was open for 4% of the time, Pallas kernels for 0%

commit v1 on v0

v1 whole, which is shorter than its diff:
```python
import functools
import jax
import jax.numpy as jnp
from jax import lax
from jax.experimental import pallas as pl
from jax.experimental.pallas import tpu as pltpu
from jax.sharding import PartitionSpec as P

highest = lax.Precision.HIGHEST
WIDE = 256
PANEL = 16


def dot(a, b, ca, cb, precision=None):
    return lax.dot_general(
        a, b, (((ca,), (cb,)), ((), ())), precision=precision, preferred_element_type=jnp.float32
    )


def partner_of(block, axis, stride):
    count = lax.axis_size(axis)
    route = [(i, i ^ (1 << stride)) for i in range(count)]
    return lax.ppermute(block, axis, route)


def sample_kernel(me_ref, dest_ref, coup_ref, upd_ref, probe_ref, rows_ref, blk_ref, pp_ref,
                  part_ref, own_ref, acc):
    step = pl.program_id(0)
    me = me_ref[0]
    high_count = acc.shape[1]
    row_blocks = rows_ref.shape[1]
    width = rows_ref.shape[2]

    @pl.when(step == 0)
    def _():
        acc[...] = jnp.zeros_like(acc)

    sampled = dot(probe_ref[...], upd_ref[0], 1, 1).astype(jnp.bfloat16)
    for b in range(row_blocks):
        rows = rows_ref[0, b : b + 1, :]
        high = lax.shift_right_logical(rows, 8)
        low = lax.bitwise_and(rows, WIDE - 1)
        spots = lax.broadcasted_iota(jnp.int32, (WIDE, width), 0)
        low_hot = jnp.where(spots == low, 1.0, 0.0).astype(jnp.bfloat16)
        part = sampled[:, b * width : (b + 1) * width]
        left = jnp.concatenate(
            [part * jnp.where(high == h, 1.0, 0.0).astype(jnp.bfloat16) for h in range(high_count)], 0
        )
        spread = dot(left, low_hot, 1, 1).reshape(acc.shape[1:])
        f = dest_ref[step * row_blocks + b]
        acc[f] += spread
    per_step = blk_ref.shape[0]
    for e in range(per_step):
        q = coup_ref[2 * (step * per_step + e)]
        s = coup_ref[2 * (step * per_step + e) + 1]
        picked = pp_ref[:, pl.ds(pl.multiple_of(s * width, width), width)]
        lane = pl.multiple_of((q % 2) * width, width)
        acc[me, q // 2, :, pl.ds(lane, width)] += dot(picked, blk_ref[e], 1, 1)

    @pl.when(step == pl.num_programs(0) - 1)
    def _():
        part_ref[...] = acc[...].astype(jnp.bfloat16)
        own_ref[...] = acc[me]


def local_samples(me, child_updates, child_probes, child_dest, child_rows, parent_blocks, coupling,
                  parent_probes, leaf_count):
    kids, order, _ = child_updates.shape
    probes = child_probes.shape[0]
    width = child_rows.shape[1]
    per_kid = order // width
    front_rows = parent_probes.shape[1]
    entries = parent_blocks.shape[0] // kids
    high = front_rows // WIDE
    rows = child_rows.reshape(kids, per_kid, width)
    grid_spec = pltpu.PrefetchScalarGridSpec(
        num_scalar_prefetch=3,
        grid=(kids,),
        in_specs=[
            pl.BlockSpec((1, order, order), lambda c, *_: (c, 0, 0)),
            pl.BlockSpec((probes, order), lambda c, *_: (0, c)),
            pl.BlockSpec((1, per_kid, width), lambda c, *_: (c, 0, 0)),
            pl.BlockSpec((entries, width, width), lambda c, *_: (c, 0, 0)),
            pl.BlockSpec((probes, front_rows), lambda c, *_: (0, 0)),
        ],
        out_specs=[
            pl.BlockSpec((leaf_count, high, probes, WIDE), lambda c, *_: (0, 0, 0, 0)),
            pl.BlockSpec((high, probes, WIDE), lambda c, *_: (0, 0, 0)),
        ],
        scratch_shapes=[pltpu.VMEM((leaf_count, high, probes, WIDE), jnp.float32)],
    )
    return pl.pallas_call(
        sample_kernel,
        grid_spec=grid_spec,
        out_shape=[
            jax.ShapeDtypeStruct((leaf_count, high, probes, WIDE), jnp.bfloat16),
            jax.ShapeDtypeStruct((high, probes, WIDE), jnp.float32),
        ],
        compiler_params=pltpu.CompilerParams(vmem_limit_bytes=56 * 1024 * 1024),
    )(me[None], child_dest.reshape(-1), coupling.reshape(-1), child_updates, child_probes, rows,
      parent_blocks, parent_probes)


def inverse_factor(work, done, gram):
    n = gram.shape[0]
    eye = lax.broadcasted_iota(jnp.int32, (n, n), 0) == lax.broadcasted_iota(jnp.int32, (n, n), 1)
    work[:, :n] = gram
    work[:, n:] = jnp.where(eye, 1.0, 0.0)
    place = lax.broadcasted_iota(jnp.int32, (PANEL, 1), 0)
    for k in range(0, n, PANEL):
        panel = work[k : k + PANEL, :]
        for j in range(PANEL):
            column = panel[:, k + j : k + j + 1]
            scale = lax.rsqrt(column[j : j + 1, :])
            row = panel[j : j + 1, :] * scale
            weight = jnp.where(place > j, column * scale, 0.0)
            panel = jnp.where(place == j, row, panel - weight * row)
        done[k : k + PANEL, :] = panel
        if k + PANEL < n:
            work[...] -= dot(panel[:, :n], panel, 0, 0, highest)
    return done[:, n:]


def basis_kernel(rank_ref, gram_ref, stack_ref, out_ref, work, done):
    inverse = inverse_factor(work, done, gram_ref[...])
    result = dot(stack_ref[...], inverse, 1, 1, highest)
    columns = lax.broadcasted_iota(jnp.int32, result.shape, 1)
    out_ref[...] = jnp.where(columns < rank_ref[0], result, 0.0)


def basis_apply(rank, gram, stack):
    n = gram.shape[0]
    return pl.pallas_call(
        basis_kernel,
        in_specs=[
            pl.BlockSpec(memory_space=pltpu.SMEM),
            pl.BlockSpec(memory_space=pltpu.VMEM),
            pl.BlockSpec(memory_space=pltpu.VMEM),
        ],
        out_specs=pl.BlockSpec(memory_space=pltpu.VMEM),
        out_shape=jax.ShapeDtypeStruct(stack.shape, jnp.float32),
        scratch_shapes=[pltpu.VMEM((n, 2 * n), jnp.float32), pltpu.VMEM((n, 2 * n), jnp.float32)],
        compiler_params=pltpu.CompilerParams(vmem_limit_bytes=24 * 1024 * 1024),
    )(rank.reshape(1), gram, stack)


def merge(passed, bit, stride, sketch, rank):
    partner = partner_of(passed, "leaf", stride)
    stacked = jnp.where(
        bit == 0,
        jnp.concatenate([passed, partner], 1),
        jnp.concatenate([partner, passed], 1),
    )
    sketched = jnp.einsum("pr,ps->rs", stacked, sketch, precision=highest)
    gram = jnp.einsum("ra,rb->ab", sketched, sketched, precision=highest)
    crossed = jnp.dot(stacked, sketched, precision=highest)
    both = basis_apply(rank, gram, jnp.concatenate([sketched, crossed], 0))
    rows = sketched.shape[0]
    return both[:rows], both[rows:]


def on_device(
    child_updates,
    child_probes,
    child_dest,
    child_rows,
    parent_blocks,
    coupling,
    parent_probes,
    sketch,
    rank_one,
    rank_two,
    rank_three,
):
    leaf_count = lax.axis_size("leaf")
    probe_count = lax.axis_size("probe")
    leaf_index = lax.axis_index("leaf")
    probe_index = lax.axis_index("probe")
    probes, front_rows = parent_probes.shape
    rank_width = sketch.shape[1]
    sketch_all = lax.all_gather(sketch, "probe", axis=0, tiled=True)
    partial, own = local_samples(
        leaf_index, child_updates, child_probes, child_dest, child_rows, parent_blocks, coupling,
        parent_probes, leaf_count,
    )
    arrived = lax.all_to_all(partial, "leaf", 0, 0, tiled=True)
    others = jnp.arange(leaf_count) != leaf_index
    sample = own + jnp.sum(
        jnp.where(others[:, None, None, None], arrived.astype(jnp.float32), 0.0), axis=0
    )
    high = front_rows // WIDE
    share = sample.astype(jnp.bfloat16).reshape(probe_count, high // probe_count, probes, WIDE)
    share = lax.all_to_all(share, "probe", 0, 0, tiled=True)
    rows_mine = jnp.moveaxis(share, 1, 2).reshape(probe_count * probes, front_rows // probe_count)
    rows_mine = rows_mine.astype(jnp.float32)
    sketched = jnp.einsum("pr,ps->rs", rows_mine, sketch_all, precision=highest)
    gram = jnp.einsum("ra,rb->ab", sketched, sketched, precision=highest)
    crossed = jnp.dot(rows_mine, sketched, precision=highest)
    sums = jnp.concatenate([gram, crossed], 0)
    stride = 0
    while 1 << stride < probe_count:
        sums = sums + partner_of(sums, "probe", stride)
        stride += 1
    both = basis_apply(
        rank_one[0], sums[:rank_width], jnp.concatenate([sketched, sums[rank_width:]], 0)
    )
    own_basis, passed_one = both[: sketched.shape[0]], both[sketched.shape[0] :]
    pair_bit = leaf_index % 2
    merged_two, passed_two = merge(passed_one, pair_bit, 0, sketch_all, rank_two[leaf_index // 2])
    quad_bit = leaf_index // 2 % 2
    merged_three, passed_three = merge(passed_two, quad_bit, 1, sketch_all, rank_three[leaf_index // 4])
    basis_two = lax.dynamic_slice_in_dim(merged_two, pair_bit * rank_width, rank_width, 0)
    basis_three = lax.dynamic_slice_in_dim(merged_three, quad_bit * rank_width, rank_width, 0)
    top = lax.dynamic_slice_in_dim(passed_three, probe_index * probes, probes, 0)
    return (own_basis, basis_two, basis_three, top)


def solution(mesh):
    return jax.shard_map(
        on_device,
        mesh=mesh,
        in_specs=(
            P("leaf", None, None),
            P("probe", "leaf"),
            P("leaf", None),
            P("leaf", None),
            P("leaf", None, None),
            P("leaf", None),
            P("probe", "leaf"),
            P("probe", None),
            P("leaf"),
            P(),
            P(),
        ),
        out_specs=(
            P(("leaf", "probe"), None),
            P("leaf", None),
            P("leaf", None),
            P("probe", "leaf"),
        ),
        check_vma=False,
    )
```

time: 416 us -> 160 us (0.38)
  other arithmetic: 172 us -> 0.69 us
  waiting for transfers between devices: 179 us -> 44.7 us
  Pallas kernels: 0 us -> 75 us
  matrix products: 31.2 us -> 4.15 us
  blocking collectives: 0 us -> 15.7 us
  between operations: 14.8 us -> 1.55 us
  local copies, waits for them, and re-layouts: 17 us -> 6.3 us
  starting transfers between devices: 2.16 us -> 11.4 us
    psum x3 -> x0, waiting for transfers between devices: 115 us -> none  [the longest x1 51.1 us: on_device(): sketched = lax.psum(partial_sketch, 'probe')]
    scatter-add x2 -> x0, other arithmetic: 98.5 us -> none  [the longest x1 91.3 us: on_device(): partial_all = jnp.zeros((local_probes, leaf_count * front_rows), jnp.floa...]
    pallas_call x0 -> x4, Pallas kernels: none -> 75 us  [the longest x3 41.4 us: basis_apply(): pl.pallas_call(basis_kernel, in_specs=[pl.BlockSpec(memory_space=pltpu.SM...]
    another operation x15 -> x0, other arithmetic: 68.6 us -> none  [the longest x9 37.2 us: basis_from_gram(): factor = jnp.linalg.cholesky(gram_matrix)]
    reduce_scatter x1 -> x0, waiting for transfers between devices: 60.8 us -> none  [on_device(): lax.psum_scatter(partial_all, 'leaf', scatter_dimension=1, tiled=True)]
    all_to_all x0 -> x2, waiting for transfers between devices: none -> 26.6 us  [the longest x1 26.6 us: on_device(): arrived = lax.all_to_all(partial, 'leaf', 0, 0, tiled=True)]
    dot_general x11 -> x9, matrix products: 26.6 us -> 4.15 us  [the longest x2 1.18 us: merge(): sketched = jnp.einsum('pr,ps->rs', stacked, sketch, precision=highest)]
    all_gather x0 -> x1, blocking collectives: none -> 15.7 us  [on_device(): sketch_all = lax.all_gather(sketch, 'probe', axis=0, tiled=True)]
  transfers between devices with their start and end apart: 6 -> 6, of which waited for: 6 -> 5; matrix products, arithmetic and copies ran while one was open for 4% -> 2% of each run, Pallas kernels for 0% -> 0%
where the time goes in v1:
time: 160 us
  Pallas kernels  75 us (47%)
  waiting for transfers between devices  44.7 us (28%)
  blocking collectives  15.7 us (10%)
  starting transfers between devices  11.4 us (7%)
  local copies, waits for them, and re-layouts  6.3 us (4%)
  matrix products  4.15 us (3%)
    pallas_call x3, Pallas kernels, basis_apply(): pl.pallas_call(basis_kernel, in_specs=[pl.BlockSpec(memory_space=pltpu.SM...  41.4 us
    pallas_call x1, Pallas kernels, local_samples(): pl.pallas_call(sample_kernel, grid_spec=grid_spec, out_shape=[jax.ShapeDt...  33.7 us
    all_to_all x1, waiting for transfers between devices, on_device(): arrived = lax.all_to_all(partial, 'leaf', 0, 0, tiled=True)  26.6 us
    ppermute x4, waiting for transfers between devices, partner_of(): return lax.ppermute(block, axis, route)  18.1 us
    all_gather x1, blocking collectives, on_device(): sketch_all = lax.all_gather(sketch, 'probe', axis=0, tiled=True)  15.7 us
    all_to_all x1, starting transfers between devices, on_device(): arrived = lax.all_to_all(partial, 'leaf', 0, 0, tiled=True)  5.19 us
    all_to_all x1, starting transfers between devices, on_device(): share = lax.all_to_all(share, 'probe', 0, 0, tiled=True)  4.87 us
  transfers between devices with their start and end apart: 6, of which 5 were waited for; matrix products, arithmetic and copies ran while one was open for 2% of the time, Pallas kernels for 0%

profile of v1, /device:TPU:0, one launch (start us, length us, event | category | flops | bytes accessed | tf_op | source)
XLA Modules:
  0.0 159.5 jit_solution(11589717276393937979)
XLA Ops:
  0.6 0.8 copy.16
  1.4 0.7 reshape.28.coup_ref
  2.1 33.7 %shard_map.138 = (bf16[8,8,64,256]{3,2,1,0:T(8,128)(2,1)}, f32[8,64,256]{2,1,0:T(8,128)}) custom-call(s32[1]{0:T(128)} %bitcast.me_ref, s32[128]{0:T(128)} %bitcast.27, s32[128]{0:T(128)} %reshape.28.coup_ref, bf16[32,512,512]{2,1,0:T(8,128)(2,1)} %upd_ref.1, bf16[64,16384]{1,0:T(8,128)(2,1)} %probe_ref.1, s32[32,4,128]{2,1,0:T(4,128)} %bitcast.26, ...), custom_call_target="tpu_custom_call" | custom-call | tf_op jit(solution)/shard_map/pallas_call | solution.py:92
  35.7 5.2 %all-to-all-start = ((bf16[8,8,64,256]{3,2,1,0:T(8,128)(2,1)}), bf16[8,8,64,256]{3,2,1,0:T(8,128)(2,1)S(1)}, u32[]{:S(2)}, u32[]{:S(2)}) async-start(bf16[8,8,64,256]{3,2,1,0:T(8,128)(2,1)} %get-tuple-element.7), calls=%async_computation | async-start | bytes 4194304 | tf_op jit(solution)/shard_map/all_to_all | solution.py:186
  40.9 0.0 copy-start
  40.9 0.0 copy-start.1
  40.9 26.6 %all-to-all-done = bf16[8,8,64,256]{3,2,1,0:T(8,128)(2,1)S(1)} async-done(((bf16[8,8,64,256]{3,2,1,0:T(8,128)(2,1)}), bf16[8,8,64,256]{3,2,1,0:T(8,128)(2,1)S(1)}, u32[]{:S(2)}, u32[]{:S(2)}) %all-to-all-start) | async-done | bytes 2097184 | tf_op jit(solution)/shard_map/all_to_all | solution.py:186
  67.6 0.5 select_reduce_fusion
  68.0 0.0 copy-done
  68.0 0.1 add_convert_fusion
  68.1 1.0 copy.17
  69.1 4.9 %all-to-all-start.1 = ((bf16[4,2,64,256]{3,1,2,0:T(2,128)(2,1)}), bf16[4,2,64,256]{3,1,2,0:T(2,128)(2,1)S(1)}, u32[]{:S(2)}, u32[]{:S(2)}) async-start(bf16[4,2,64,256]{3,1,2,0:T(2,128)(2,1)} %copy.17), calls=%async_computation.1 | async-start | bytes 524288 | tf_op jit(solution)/shard_map/all_to_all | solution.py:193
  74.0 0.0 copy-done.1
  74.0 15.7 %all_gather.3 = f32[256,128]{1,0:T(8,128)S(1)} all-gather(f32[64,128]{1,0:T(8,128)S(1)} %copy-done.1), channel_id=1, replica_groups=mesh['leaf'=8,'probe'=4] {'probe'}, dimensions={0}, use_global_device_ids=true | all-gather | bytes 163840 | tf_op jit(solution)/shard_map/all_gather | solution.py:181
  89.7 0.0 all-to-all-done.1
  89.7 0.5 fusion.15
  90.2 0.4 fusion.17
  90.6 0.6 fusion.16
  91.2 0.0 copy-start.2
  91.2 0.3 collective-permute-start
  91.5 7.5 %collective-permute-done = f32[384,128]{1,0:T(8,128)S(1)} collective-permute-done((f32[384,128]{1,0:T(8,128)S(1)}, f32[384,128]{1,0:T(8,128)S(1)}, u32[]{:S(2)}, u32[]{:S(2)}) %collective-permute-start) | collective-permute-done | bytes 196640 | tf_op jit(solution)/shard_map/ppermute | solution.py:23
  99.0 0.3 collective-permute-start.1
  99.9 7.0 %collective-permute-done.1 = f32[384,128]{1,0:T(8,128)S(1)} collective-permute-done((f32[384,128]{1,0:T(8,128)S(1)}, f32[384,128]{1,0:T(8,128)S(1)}, u32[]{:S(2)}, u32[]{:S(2)}) %collective-permute-start.1) | collective-permute-done | bytes 196640 | tf_op jit(solution)/shard_map/ppermute | solution.py:23
  107.0 0.0 copy-start.3
  107.0 13.4 %shard_map.139 = f32[768,128]{1,0:T(8,128)S(1)} custom-call(s32[1]{0:T(128)S(6)} %copy.19.rank_ref, f32[128,128]{1,0:T(8,128)S(1)} %slice.32.gram_ref, f32[768,128]{1,0:T(8,128)S(1)} %pad_maximum_fusion.stack_ref), custom_call_target="tpu_custom_call" | custom-call | tf_op jit(solution)/shard_map/pallas_call | solution.py:133
  120.4 0.1 collective-permute-start.2
  120.6 0.0 copy-done.2
  120.6 0.6 dynamic_slice.15.rank_ref
  121.2 0.7 collective-permute-done.2
  121.9 0.6 fusion.3
  122.5 0.4 fusion.18.gram_ref
  122.8 0.4 fusion.2
  123.3 14.0 %shard_map.140 = f32[512,128]{1,0:T(8,128)S(1)} custom-call(s32[1]{0:T(128)} %dynamic_slice.15.rank_ref, f32[128,128]{1,0:T(8,128)S(1)} %fusion.18.gram_ref, f32[512,128]{1,0:T(8,128)S(1)} %pad_maximum_fusion.1.stack_ref), custom_call_target="tpu_custom_call" | custom-call | tf_op jit(solution)/shard_map/pallas_call | solution.py:133
  137.3 0.8 collective-permute-start.3
  138.1 0.0 copy-done.3
  138.1 0.6 dynamic_slice.17.rank_ref
  138.6 0.7 slice.34
  139.4 0.6 constant_dynamic-slice_fusion.2
  140.0 2.9 %collective-permute-done.3 = f32[256,128]{1,0:T(8,128)S(1)} collective-permute-done((f32[256,128]{1,0:T(8,128)S(1)}, f32[256,128]{1,0:T(8,128)S(1)}, u32[]{:S(2)}, u32[]{:S(2)}) %collective-permute-start.3) | collective-permute-done | bytes 131104 | tf_op jit(solution)/shard_map/ppermute | solution.py:23
  142.9 0.6 fusion.1
  143.5 0.4 fusion.19.gram_ref
  143.9 0.4 fusion
  144.3 14.0 %shard_map.141 = f32[512,128]{1,0:T(8,128)S(1)} custom-call(s32[1]{0:T(128)} %dynamic_slice.17.rank_ref, f32[128,128]{1,0:T(8,128)S(1)} %fusion.19.gram_ref, f32[512,128]{1,0:T(8,128)S(1)} %pad_maximum_fusion.2.stack_ref), custom_call_target="tpu_custom_call" | custom-call | tf_op jit(solution)/shard_map/pallas_call | solution.py:133
  158.3 0.6 constant_dynamic-slice_fusion.1
  158.9 0.6 constant_dynamic-slice_fusion
  (13 shorter events, 0.2 us)
Async XLA Ops:
  35.7 31.8 %all-to-all-start = ((bf16[8,8,64,256]{3,2,1,0:T(8,128)(2,1)}), bf16[8,8,64,256]{3,2,1,0:T(8,128)(2,1)S(1)}, u32[]{:S(2)}, u32[]{:S(2)}) async-start(bf16[8,8,64,256]{3,2,1,0:T(8,128)(2,1)} %get-tuple-element.7), calls=%async_computation | async-start | bytes 4194304 | tf_op jit(solution)/shard_map/all_to_all | solution.py:186
  40.9 27.1 %copy-start = (f32[8,64,256]{2,1,0:T(8,128)S(1)}, f32[8,64,256]{2,1,0:T(8,128)}, u32[]{:S(2)}) copy-start(f32[8,64,256]{2,1,0:T(8,128)} %get-tuple-element.6) | copy-start | bytes 1572868
  40.9 33.0 %copy-start.1 = (f32[64,128]{1,0:T(8,128)S(1)}, f32[64,128]{1,0:T(8,128)}, u32[]{:S(2)}) copy-start(f32[64,128]{1,0:T(8,128)} %param.18) | copy-start | bytes 98308
  69.1 20.6 %all-to-all-start.1 = ((bf16[4,2,64,256]{3,1,2,0:T(2,128)(2,1)}), bf16[4,2,64,256]{3,1,2,0:T(2,128)(2,1)S(1)}, u32[]{:S(2)}, u32[]{:S(2)}) async-start(bf16[4,2,64,256]{3,1,2,0:T(2,128)(2,1)} %copy.17), calls=%async_computation.1 | async-start | bytes 524288 | tf_op jit(solution)/shard_map/all_to_all | solution.py:193
  91.2 29.4 %copy-start.2 = (s32[4]{0:T(128)S(1)}, s32[4]{0:T(128)}, u32[]{:S(2)}) copy-start(s32[4]{0:T(128)} %param.20) | copy-start | bytes 52
  91.2 7.7 %collective-permute-start = (f32[384,128]{1,0:T(8,128)S(1)}, f32[384,128]{1,0:T(8,128)S(1)}, u32[]{:S(2)}, u32[]{:S(2)}) collective-permute-start(f32[384,128]{1,0:T(8,128)S(1)} %pad_maximum_fusion.3), channel_id=1, source_target_pairs={{0,1},{1,0},{2,3},{3,2},{4,5},{5,4},{6,7},{7,6},{8,9},{9,8},{10,11... | collective-permute-start | bytes 589832 | tf_op jit(solution)/shard_map/ppermute | solution.py:23
  99.0 7.9 %collective-permute-start.1 = (f32[384,128]{1,0:T(8,128)S(1)}, f32[384,128]{1,0:T(8,128)S(1)}, u32[]{:S(2)}, u32[]{:S(2)}) collective-permute-start(f32[384,128]{1,0:T(8,128)S(1)} %fusion.12), channel_id=1, source_target_pairs={{0,2},{1,3},{2,0},{3,1},{4,6},{5,7},{6,4},{7,5},{8,10},{9,11},{10,... | collective-permute-start | bytes 589832 | tf_op jit(solution)/shard_map/ppermute | solution.py:23
  107.0 31.1 %copy-start.3 = (s32[2]{0:T(128)S(1)}, s32[2]{0:T(128)}, u32[]{:S(2)}) copy-start(s32[2]{0:T(128)} %param.21) | copy-start | bytes 28
  120.4 1.4 collective-permute-start.2
  137.3 5.6 %collective-permute-start.3 = (f32[256,128]{1,0:T(8,128)S(1)}, f32[256,128]{1,0:T(8,128)S(1)}, u32[]{:S(2)}, u32[]{:S(2)}) collective-permute-start(f32[256,128]{1,0:T(8,128)S(1)} %get-tuple-element.10), channel_id=1, source_target_pairs={{0,8},{4,12},{8,0},{12,4},{16,24},{20,28},{24,16},{28,20},{1,9},{5... | collective-permute-start | bytes 393224 | tf_op jit(solution)/shard_map/ppermute | solution.py:23

commit v2 on v1

v2 whole, which is shorter than its diff:
```python
import functools
import jax
import jax.numpy as jnp
from jax import lax
from jax.experimental import pallas as pl
from jax.experimental.pallas import tpu as pltpu
from jax.sharding import PartitionSpec as P

highest = lax.Precision.HIGHEST
WIDE = 256
PANEL = 16
KIDS = 2


def dot(a, b, ca, cb, precision=None):
    return lax.dot_general(
        a, b, (((ca,), (cb,)), ((), ())), precision=precision, preferred_element_type=jnp.float32
    )


def partner_of(block, axis, stride):
    count = lax.axis_size(axis)
    route = [(i, i ^ (1 << stride)) for i in range(count)]
    return lax.ppermute(block, axis, route)


def gathered(block, axis):
    count = lax.axis_size(axis)
    index = lax.axis_index(axis)
    rows = block.shape[0]
    result = jnp.zeros((count * rows,) + block.shape[1:], block.dtype)
    result = lax.dynamic_update_slice_in_dim(result, block, index * rows, 0)
    for shift in range(1, count):
        came = lax.ppermute(block, axis, [(i, (i + shift) % count) for i in range(count)])
        source = (index - shift + count) % count
        result = lax.dynamic_update_slice_in_dim(result, came, source * rows, 0)
    return result


def sample_kernel(dest_ref, coup_ref, upd_ref, probe_ref, rows_ref, blk_ref, pp_ref,
                  send_ref, keep_ref, acc):
    step = pl.program_id(0)
    me = lax.axis_index("leaf")
    high_count = acc.shape[1]
    kids, row_blocks, width = rows_ref.shape
    order = upd_ref.shape[1]

    @pl.when(step == 0)
    def _():
        acc[...] = jnp.zeros_like(acc)

    spots = lax.broadcasted_iota(jnp.int32, (WIDE, width), 0)
    sampled = [
        dot(probe_ref[:, c * order : (c + 1) * order], upd_ref[c], 1, 1).astype(jnp.bfloat16)
        for c in range(kids)
    ]
    for c in range(kids):
        for b in range(row_blocks):
            rows = rows_ref[c, b : b + 1, :]
            high = lax.shift_right_logical(rows, 8)
            low = lax.bitwise_and(rows, WIDE - 1)
            low_hot = jnp.where(spots == low, 1.0, 0.0).astype(jnp.bfloat16)
            part = sampled[c][:, b * width : (b + 1) * width]
            left = jnp.concatenate(
                [
                    part * jnp.where(high == h, 1.0, 0.0).astype(jnp.bfloat16)
                    for h in range(high_count)
                ],
                0,
            )
            spread = dot(left, low_hot, 1, 1).reshape(acc.shape[1:])
            f = dest_ref[(step * kids + c) * row_blocks + b]
            acc[f] += spread
    per_step = blk_ref.shape[0]
    for e in range(per_step):
        q = coup_ref[2 * (step * per_step + e)]
        s = coup_ref[2 * (step * per_step + e) + 1]
        picked = pp_ref[:, pl.ds(pl.multiple_of(s * width, width), width)]
        lane = pl.multiple_of((q % 2) * width, width)
        acc[me, q // 2, :, pl.ds(lane, width)] += dot(picked, blk_ref[e], 1, 1)

    @pl.when(step == pl.num_programs(0) - 1)
    def _():
        bit = me % 2
        for i in range(send_ref.shape[0]):
            send_ref[i] = acc[2 * i + 1 - bit].astype(jnp.bfloat16)
            keep_ref[i] = acc[2 * i + bit]


def local_samples(child_updates, child_probes, child_dest, child_rows, parent_blocks, coupling,
                  parent_probes, leaf_count):
    kids, order, _ = child_updates.shape
    probes = child_probes.shape[0]
    width = child_rows.shape[1]
    per_kid = order // width
    front_rows = parent_probes.shape[1]
    steps = kids // KIDS
    entries = parent_blocks.shape[0] // steps
    high = front_rows // WIDE
    half = leaf_count // 2
    rows = child_rows.reshape(kids, per_kid, width)
    grid_spec = pltpu.PrefetchScalarGridSpec(
        num_scalar_prefetch=2,
        grid=(steps,),
        in_specs=[
            pl.BlockSpec((KIDS, order, order), lambda c, *_: (c, 0, 0)),
            pl.BlockSpec((probes, KIDS * order), lambda c, *_: (0, c)),
            pl.BlockSpec((KIDS, per_kid, width), lambda c, *_: (c, 0, 0)),
            pl.BlockSpec((entries, width, width), lambda c, *_: (c, 0, 0)),
            pl.BlockSpec((probes, front_rows), lambda c, *_: (0, 0)),
        ],
        out_specs=[
            pl.BlockSpec((half, high, probes, WIDE), lambda c, *_: (0, 0, 0, 0)),
            pl.BlockSpec((half, high, probes, WIDE), lambda c, *_: (0, 0, 0, 0)),
        ],
        scratch_shapes=[pltpu.VMEM((leaf_count, high, probes, WIDE), jnp.float32)],
    )
    return pl.pallas_call(
        sample_kernel,
        grid_spec=grid_spec,
        out_shape=[
            jax.ShapeDtypeStruct((half, high, probes, WIDE), jnp.bfloat16),
            jax.ShapeDtypeStruct((half, high, probes, WIDE), jnp.float32),
        ],
        compiler_params=pltpu.CompilerParams(vmem_limit_bytes=56 * 1024 * 1024),
    )(child_dest.reshape(-1), coupling.reshape(-1), child_updates, child_probes, rows,
      parent_blocks, parent_probes)


def halve(values, index, bits):
    rest = list(bits)
    for bit in bits:
        ordered = sorted(rest, reverse=True)
        spot = ordered.index(bit)
        mine = index // (1 << bit) % 2
        kept = lax.dynamic_index_in_dim(values, mine, spot, keepdims=False)
        sent = lax.dynamic_index_in_dim(values, 1 - mine, spot, keepdims=False)
        came = partner_of(sent.astype(jnp.bfloat16), "leaf", bit)
        values = kept + came.astype(jnp.float32)
        rest.remove(bit)
    return values


def inverse_factor(work_u, work_v, done, gram):
    n = gram.shape[0]
    eye = lax.broadcasted_iota(jnp.int32, (n, n), 0) == lax.broadcasted_iota(jnp.int32, (n, n), 1)
    work_u[...] = gram
    work_v[...] = jnp.where(eye, 1.0, 0.0)
    place = lax.broadcasted_iota(jnp.int32, (PANEL, n), 0)
    for k in range(0, n, PANEL):
        left = work_u[k : k + PANEL, :]
        right = work_v[k : k + PANEL, :]
        for j in range(PANEL):
            column = jnp.broadcast_to(left[:, k + j : k + j + 1], (PANEL, n))
            scale = lax.rsqrt(column[j : j + 1, :])
            row_u = left[j : j + 1, :] * scale
            row_v = right[j : j + 1, :] * scale
            weight = jnp.where(place > j, column * scale, 0.0)
            left = jnp.where(place == j, row_u, left - weight * row_u)
            right = jnp.where(place == j, row_v, right - weight * row_v)
        done[k : k + PANEL, :] = right
        if k + PANEL < n:
            work_u[...] -= dot(left, left, 0, 0, highest)
            work_v[...] -= dot(left, right, 0, 0, highest)
    return done[...]


def limited(stack, inverse, rank):
    result = dot(stack, inverse, 1, 1, highest)
    columns = lax.broadcasted_iota(jnp.int32, result.shape, 1)
    return jnp.where(columns < rank, result, 0.0)


def front_kernel(rank_ref, sums_ref, sketched_ref, basis_ref, passed_ref, work_u, work_v, done):
    n = done.shape[0]
    inverse = inverse_factor(work_u, work_v, done, sums_ref[:n])
    passed_ref[...] = limited(sums_ref[n:], inverse, rank_ref[0])
    basis_ref[...] = limited(sketched_ref[...], inverse, rank_ref[0])


def merge_kernel(stride, rank_ref, own_ref, partner_ref, sketch_ref, basis_ref, passed_ref,
                 work_u, work_v, done):
    leaf = lax.axis_index("leaf")
    bit = leaf // (1 << stride) % 2
    rank = rank_ref[leaf // (2 << stride)]
    n = done.shape[0]
    own = own_ref[...]
    partner = partner_ref[...]
    stacked = jnp.concatenate(
        [jnp.where(bit == 0, own, partner), jnp.where(bit == 0, partner, own)], 1
    )
    sketched = dot(stacked, sketch_ref[...], 0, 0, highest)
    gram = dot(sketched, sketched, 0, 0, highest)
    crossed = dot(stacked, sketched, 1, 0, highest)
    inverse = inverse_factor(work_u, work_v, done, gram)
    passed_ref[...] = limited(crossed, inverse, rank)
    basis_ref[...] = limited(jnp.where(bit == 0, sketched[:n], sketched[n:]), inverse, rank)


def basis_call(kernel, outs, n, *operands):
    return pl.pallas_call(
        kernel,
        in_specs=[pl.BlockSpec(memory_space=pltpu.SMEM)]
        + [pl.BlockSpec(memory_space=pltpu.VMEM)] * (len(operands) - 1),
        out_specs=[pl.BlockSpec(memory_space=pltpu.VMEM)] * len(outs),
        out_shape=[jax.ShapeDtypeStruct(shape, jnp.float32) for shape in outs],
        scratch_shapes=[pltpu.VMEM((n, n), jnp.float32)] * 3,
        compiler_params=pltpu.CompilerParams(vmem_limit_bytes=24 * 1024 * 1024),
    )(*operands)


def merge(passed, stride, sketch, ranks):
    n = sketch.shape[1]
    partner = partner_of(passed, "leaf", stride)
    return basis_call(
        functools.partial(merge_kernel, stride), [(n, n), passed.shape], n,
        ranks, passed, partner, sketch,
    )


def on_device(
    child_updates,
    child_probes,
    child_dest,
    child_rows,
    parent_blocks,
    coupling,
    parent_probes,
    sketch,
    rank_one,
    rank_two,
    rank_three,
):
    leaf_count = lax.axis_size("leaf")
    probe_count = lax.axis_size("probe")
    leaf_index = lax.axis_index("leaf")
    probe_index = lax.axis_index("probe")
    probes, front_rows = parent_probes.shape
    rank_width = sketch.shape[1]
    high = front_rows // WIDE
    sketch_all = gathered(sketch, "probe")
    send, keep = local_samples(
        child_updates, child_probes, child_dest, child_rows, parent_blocks, coupling,
        parent_probes, leaf_count,
    )
    bits = leaf_count.bit_length() - 1
    summed = keep + partner_of(send, "leaf", 0).astype(jnp.float32)
    summed = summed.reshape((2,) * (bits - 1) + keep.shape[1:])
    rising = list(range(1, bits))
    cut = [slice(None)] * (bits - 1)
    halves = [
        halve(summed[tuple(cut + [slice(0, high // 2)])], leaf_index, rising),
        halve(summed[tuple(cut + [slice(high // 2, high)])], leaf_index, rising[::-1]),
    ]
    sample = jnp.concatenate(halves, 0)
    share = sample.astype(jnp.bfloat16).reshape(probe_count, high // probe_count, probes, WIDE)
    share = lax.all_to_all(share, "probe", 0, 0, tiled=True)
    rows_mine = jnp.moveaxis(share, 1, 2).reshape(probe_count * probes, front_rows // probe_count)
    rows_mine = rows_mine.astype(jnp.float32)
    sketched = jnp.einsum("pr,ps->rs", rows_mine, sketch_all, precision=highest)
    gram = jnp.einsum("ra,rb->ab", sketched, sketched, precision=highest)
    crossed = jnp.dot(rows_mine, sketched, precision=highest)
    sums = jnp.concatenate([gram, crossed], 0)
    stride = 0
    while 1 << stride < probe_count:
        sums = sums + partner_of(sums, "probe", stride)
        stride += 1
    own_basis, passed_one = basis_call(
        front_kernel, [sketched.shape, crossed.shape], rank_width, rank_one, sums, sketched
    )
    basis_two, passed_two = merge(passed_one, 0, sketch_all, rank_two)
    basis_three, passed_three = merge(passed_two, 1, sketch_all, rank_three)
    top = lax.dynamic_slice_in_dim(passed_three, probe_index * probes, probes, 0)
    return (own_basis, basis_two, basis_three, top)


def solution(mesh):
    return jax.shard_map(
        on_device,
        mesh=mesh,
        in_specs=(
            P("leaf", None, None),
            P("probe", "leaf"),
            P("leaf", None),
            P("leaf", None),
            P("leaf", None, None),
            P("leaf", None),
            P("probe", "leaf"),
            P("probe", None),
            P("leaf"),
            P(),
            P(),
        ),
        out_specs=(
            P(("leaf", "probe"), None),
            P("leaf", None),
            P("leaf", None),
            P("probe", "leaf"),
        ),
        check_vma=False,
    )
```

time: 160 us -> 135 us (0.84)
  blocking collectives: 15.7 us -> 0 us
  starting transfers between devices: 11.4 us -> 21.1 us
  waiting for transfers between devices: 44.7 us -> 36.9 us
  Pallas kernels: 75 us -> 67.4 us
  local copies, waits for them, and re-layouts: 6.3 us -> 2.74 us
  matrix products: 4.15 us -> 1.44 us
  other arithmetic: 0.69 us -> 2.86 us
    all_to_all x1 -> x0, waiting for transfers between devices: 26.6 us -> none  [on_device(): arrived = lax.all_to_all(partial, 'leaf', 0, 0, tiled=True)]
    all_gather x1 -> x0, blocking collectives: 15.7 us -> none  [on_device(): sketch_all = lax.all_gather(sketch, 'probe', axis=0, tiled=True)]
    ppermute x4 -> x9, waiting for transfers between devices: 18.1 us -> 30.4 us  [partner_of(): return lax.ppermute(block, axis, route)]
    ppermute x4 -> x9, starting transfers between devices: 1.39 us -> 12 us  [partner_of(): return lax.ppermute(block, axis, route)]
    pallas_call x1, Pallas kernels: 33.7 us -> 24.1 us  [local_samples(): pl.pallas_call(sample_kernel, grid_spec=grid_spec, out_shape=[jax.ShapeDt...]
    all_to_all x1, waiting for transfers between devices: 0.01 us -> 6.48 us  [on_device(): share = lax.all_to_all(share, 'probe', 0, 0, tiled=True)]
    ppermute x0 -> x3, starting transfers between devices: none -> 5.51 us  [gathered(): lax.ppermute(block, axis, [(i, (i + shift) % count) for i in range(count)])]
    all_to_all x1 -> x0, starting transfers between devices: 5.19 us -> none  [on_device(): arrived = lax.all_to_all(partial, 'leaf', 0, 0, tiled=True)]
  transfers between devices with their start and end apart: 6 -> 13, of which waited for: 5 -> 9; matrix products, arithmetic and copies ran while one was open for 2% -> 1% of each run, Pallas kernels for 0% -> 0%
where the time goes in v2:
time: 135 us; the launch traced here: 134 us
  Pallas kernels  67.4 us (50%)
  waiting for transfers between devices  36.9 us (27%)
  starting transfers between devices  21.1 us (16%)
  other arithmetic  2.86 us (2%)
  local copies, waits for them, and re-layouts  2.74 us (2%)
  between operations  1.54 us (1%)
  matrix products  1.44 us (1%)
    pallas_call x3, Pallas kernels, basis_call(): pl.pallas_call(kernel, in_specs=[pl.BlockSpec(memory_space=pltpu.SMEM)] +...  43.3 us
    ppermute x9, waiting for transfers between devices, partner_of(): return lax.ppermute(block, axis, route)  30.4 us
    pallas_call x1, Pallas kernels, local_samples(): pl.pallas_call(sample_kernel, grid_spec=grid_spec, out_shape=[jax.ShapeDt...  24.1 us
    ppermute x9, starting transfers between devices, partner_of(): return lax.ppermute(block, axis, route)  12 us
    all_to_all x1, waiting for transfers between devices, on_device(): share = lax.all_to_all(share, 'probe', 0, 0, tiled=True)  6.48 us
    ppermute x3, starting transfers between devices, gathered(): lax.ppermute(block, axis, [(i, (i + shift) % count) for i in range(count)])  5.51 us
    all_to_all x1, starting transfers between devices, on_device(): share = lax.all_to_all(share, 'probe', 0, 0, tiled=True)  3.59 us
  transfers between devices with their start and end apart: 13, of which 9 were waited for; matrix products, arithmetic and copies ran while one was open for 1% of the time, Pallas kernels for 0%

profile of v2, /device:TPU:0, one launch (start us, length us, event | category | flops | bytes accessed | tf_op | source)
XLA Modules:
  0.0 133.9 jit_solution(13383600359107749868)
XLA Ops:
  0.6 0.8 copy.19
  1.4 0.7 reshape.31.coup_ref
  2.1 24.1 %shard_map.138 = (bf16[4,8,64,256]{3,2,1,0:T(8,128)(2,1)}, f32[4,8,64,256]{3,2,1,0:T(8,128)}) custom-call(s32[128]{0:T(128)} %bitcast.40, s32[128]{0:T(128)} %reshape.31.coup_ref, bf16[32,512,512]{2,1,0:T(8,128)(2,1)} %upd_ref.1, bf16[64,16384]{1,0:T(8,128)(2,1)} %probe_ref.1, s32[32,4,128]{2,1,0:T(4,128)} %bitcast.39, bf16[64,128,128]{2,1,0:T(8,128)(2,1)} %blk_ref.1, ...), custom_call_target="tpu_custom_call" | custom-call | tf_op jit(solution)/shard_map/pallas_call | solution.py:118
  26.2 0.4 collective-permute-start
  26.6 2.5 %collective-permute-done = bf16[4,8,64,256]{3,2,1,0:T(8,128)(2,1)S(1)} collective-permute-done((bf16[4,8,64,256]{3,2,1,0:T(8,128)(2,1)}, bf16[4,8,64,256]{3,2,1,0:T(8,128)(2,1)S(1)}, u32[]{:S(2)}, u32[]{:S(2)}) %collective-permute-start) | collective-permute-done | bytes 1048608 | tf_op jit(solution)/shard_map/ppermute | solution.py:24
  29.1 1.9 %convert_add_fusion = f32[4,8,64,256]{3,2,1,0:T(8,128)S(1)} fusion(f32[4,8,64,256]{3,2,1,0:T(8,128)} %get-tuple-element.12, bf16[4,8,64,256]{3,2,1,0:T(8,128)(2,1)S(1)} %collective-permute-done), kind=kLoop, calls=%fused_computation | loop fusion | flops 1048576 | bytes 5242880 | tf_op jit(solution)/shard_map/add | solution.py:247
  31.0 0.0 copy-start.2
  31.0 0.2 fusion.7
  31.3 3.0 %collective-permute-start.3 = (bf16[2,4,64,256]{3,2,1,0:T(8,128)(2,1)S(1)}, bf16[2,4,64,256]{3,2,1,0:T(8,128)(2,1)S(1)}, u32[]{:S(2)}, u32[]{:S(2)}) collective-permute-start(bf16[2,4,64,256]{3,2,1,0:T(8,128)(2,1)S(1)} %fusion.1), channel_id=1, source_target_pairs={{0,16},{4,20},{8,24},{12,28},{16,0},{20,4},{24,8},{28,12},{1,17},{... | collective-permute-start | bytes 786440 | tf_op jit(solution)/shard_map/ppermute | solution.py:24
  34.3 0.0 copy-done.2
  34.3 1.6 %collective-permute-start.5 = (f32[64,128]{1,0:T(8,128)S(1)}, f32[64,128]{1,0:T(8,128)S(1)}, u32[]{:S(2)}, u32[]{:S(2)}) collective-permute-start(f32[64,128]{1,0:T(8,128)S(1)} %copy-done.2), channel_id=1, source_target_pairs={{0,1},{1,2},{2,3},{3,0},{4,5},{5,6},{6,7},{7,4},{8,9},{9,10},{10,1... | collective-permute-start | bytes 98312 | tf_op jit(solution)/shard_map/ppermute | solution.py:34
  35.8 2.6 %collective-permute-start.6 = (f32[64,128]{1,0:T(8,128)S(1)}, f32[64,128]{1,0:T(8,128)S(1)}, u32[]{:S(2)}, u32[]{:S(2)}) collective-permute-start(f32[64,128]{1,0:T(8,128)S(1)} %copy-done.2), channel_id=1, source_target_pairs={{0,2},{1,3},{2,0},{3,1},{4,6},{5,7},{6,4},{7,5},{8,10},{9,11},{10,... | collective-permute-start | bytes 98312 | tf_op jit(solution)/shard_map/ppermute | solution.py:34
  38.4 1.3 %collective-permute-start.7 = (f32[64,128]{1,0:T(8,128)S(1)}, f32[64,128]{1,0:T(8,128)S(1)}, u32[]{:S(2)}, u32[]{:S(2)}) collective-permute-start(f32[64,128]{1,0:T(8,128)S(1)} %copy-done.2), channel_id=1, source_target_pairs={{0,3},{1,0},{2,1},{3,2},{4,7},{5,4},{6,5},{7,6},{8,11},{9,8},{10,9... | collective-permute-start | bytes 98312 | tf_op jit(solution)/shard_map/ppermute | solution.py:34
  39.8 1.6 %collective-permute-start.1 = (bf16[2,4,64,256]{3,2,1,0:T(8,128)(2,1)S(1)}, bf16[2,4,64,256]{3,2,1,0:T(8,128)(2,1)S(1)}, u32[]{:S(2)}, u32[]{:S(2)}) collective-permute-start(bf16[2,4,64,256]{3,2,1,0:T(8,128)(2,1)S(1)} %fusion), channel_id=1, source_target_pairs={{0,8},{4,12},{8,0},{12,4},{16,24},{20,28},{24,16},{28,20},{1,9},{5... | collective-permute-start | bytes 786440 | tf_op jit(solution)/shard_map/ppermute | solution.py:24
  41.4 0.0 collective-permute-done.3
  41.4 0.1 bitcast_add_fusion
  41.5 1.3 collective-permute-start.4
  42.7 5.8 %collective-permute-done.1 = bf16[2,4,64,256]{3,2,1,0:T(8,128)(2,1)S(1)} collective-permute-done((bf16[2,4,64,256]{3,2,1,0:T(8,128)(2,1)S(1)}, bf16[2,4,64,256]{3,2,1,0:T(8,128)(2,1)S(1)}, u32[]{:S(2)}, u32[]{:S(2)}) %collective-permute-start.1) | collective-permute-done | bytes 262176 | tf_op jit(solution)/shard_map/ppermute | solution.py:24
  48.5 0.1 bitcast_add_fusion.1
  48.6 0.8 collective-permute-start.2
  49.4 0.5 collective-permute-done.4
  49.9 3.7 %collective-permute-done.2 = bf16[4,64,256]{2,1,0:T(8,128)(2,1)S(1)} collective-permute-done((bf16[4,64,256]{2,1,0:T(8,128)(2,1)S(1)}, bf16[4,64,256]{2,1,0:T(8,128)(2,1)S(1)}, u32[]{:S(2)}, u32[]{:S(2)}) %collective-permute-start.2) | collective-permute-done | bytes 131104 | tf_op jit(solution)/shard_map/ppermute | solution.py:24
  53.7 0.7 pad_maximum_fusion
  54.4 3.6 %all-to-all-start = ((bf16[4,2,64,256]{3,2,1,0:T(8,128)(2,1)}), bf16[4,2,64,256]{3,2,1,0:T(8,128)(2,1)S(1)}, u32[]{:S(2)}, u32[]{:S(2)}) async-start(bf16[4,2,64,256]{3,2,1,0:T(8,128)(2,1)} %bitcast.11), calls=%async_computation | async-start | bytes 524288 | tf_op jit(solution)/shard_map/all_to_all | solution.py:257
  58.1 0.0 collective-permute-done.5
  58.1 0.0 collective-permute-done.6
  58.1 0.0 collective-permute-done.7
  58.2 6.5 %all-to-all-done = bf16[4,2,64,256]{3,2,1,0:T(8,128)(2,1)S(1)} async-done(((bf16[4,2,64,256]{3,2,1,0:T(8,128)(2,1)}), bf16[4,2,64,256]{3,2,1,0:T(8,128)(2,1)S(1)}, u32[]{:S(2)}, u32[]{:S(2)}) %all-to-all-start) | async-done | bytes 262176 | tf_op jit(solution)/shard_map/all_to_all | solution.py:257
  64.6 0.3 copy.20
  65.0 0.0 copy-start
  65.0 0.0 copy-start.1
  65.0 0.5 fusion.8.sketched_ref
  65.4 0.4 fusion.10
  65.8 0.6 fusion.9
  66.5 2.8 %collective-permute-start.8 = (f32[384,128]{1,0:T(8,128)S(1)}, f32[384,128]{1,0:T(8,128)S(1)}, u32[]{:S(2)}, u32[]{:S(2)}) collective-permute-start(f32[384,128]{1,0:T(8,128)S(1)} %pad_maximum_fusion.1), channel_id=1, source_target_pairs={{0,1},{1,0},{2,3},{3,2},{4,5},{5,4},{6,7},{7,6},{8,9},{9,8},{10,11... | collective-permute-start | bytes 589832 | tf_op jit(solution)/shard_map/ppermute | solution.py:24
  69.2 5.3 %collective-permute-done.8 = f32[384,128]{1,0:T(8,128)S(1)} collective-permute-done((f32[384,128]{1,0:T(8,128)S(1)}, f32[384,128]{1,0:T(8,128)S(1)}, u32[]{:S(2)}, u32[]{:S(2)}) %collective-permute-start.8) | collective-permute-done | bytes 196640 | tf_op jit(solution)/shard_map/ppermute | solution.py:24
  74.6 0.7 collective-permute-start.9
  75.9 7.2 %collective-permute-done.9 = f32[384,128]{1,0:T(8,128)S(1)} collective-permute-done((f32[384,128]{1,0:T(8,128)S(1)}, f32[384,128]{1,0:T(8,128)S(1)}, u32[]{:S(2)}, u32[]{:S(2)}) %collective-permute-start.9) | collective-permute-done | bytes 196640 | tf_op jit(solution)/shard_map/ppermute | solution.py:24
  83.1 13.6 %shard_map.139 = (f32[512,128]{1,0:T(8,128)}, f32[256,128]{1,0:T(8,128)S(1)}) custom-call(s32[1]{0:T(128)S(6)} %copy.26.rank_ref, f32[384,128]{1,0:T(8,128)S(1)} %add.115.sums_ref, f32[512,128]{1,0:T(8,128)S(1)} %fusion.8.sketched_ref), custom_call_target="tpu_custom_call" | custom-call | tf_op jit(solution)/shard_map/pallas_call | solution.py:201
  96.7 0.0 collective-permute-start.10
  96.7 1.3 %collective-permute-done.10.partner_ref = f32[256,128]{1,0:T(8,128)S(1)} collective-permute-done((f32[256,128]{1,0:T(8,128)S(1)}, f32[256,128]{1,0:T(8,128)S(1)}, u32[]{:S(2)}, u32[]{:S(2)}) %collective-permute-start.10) | collective-permute-done | bytes 131104 | tf_op jit(solution)/shard_map/ppermute | solution.py:24
  98.1 0.0 copy-done
  98.1 14.8 %shard_map.140 = (f32[128,128]{1,0:T(8,128)}, f32[256,128]{1,0:T(8,128)S(1)}) custom-call(s32[4]{0:T(128)S(1)} %copy-done, f32[256,128]{1,0:T(8,128)S(1)} %get-tuple-element.15.own_ref, f32[256,128]{1,0:T(8,128)S(1)} %collective-permute-done.10.partner_ref, f32[256,128]{1,0:T(8,128)S(1)} %constant_dynamic-update-slice_fusion.sketch_ref), custom_call_target="tpu_custom_call" | custom-call | tf_op jit(solution)/shard_map/pallas_call | solution.py:201
  112.9 1.5 %collective-permute-start.11 = (f32[256,128]{1,0:T(8,128)S(1)}, f32[256,128]{1,0:T(8,128)S(1)}, u32[]{:S(2)}, u32[]{:S(2)}) collective-permute-start(f32[256,128]{1,0:T(8,128)S(1)} %get-tuple-element.17.own_ref), channel_id=1, source_target_pairs={{0,8},{4,12},{8,0},{12,4},{16,24},{20,28},{24,16},{28,20},{1,9},{5... | collective-permute-start | bytes 393224 | tf_op jit(solution)/shard_map/ppermute | solution.py:24
  114.4 4.1 %collective-permute-done.11.partner_ref = f32[256,128]{1,0:T(8,128)S(1)} collective-permute-done((f32[256,128]{1,0:T(8,128)S(1)}, f32[256,128]{1,0:T(8,128)S(1)}, u32[]{:S(2)}, u32[]{:S(2)}) %collective-permute-start.11) | collective-permute-done | bytes 131104 | tf_op jit(solution)/shard_map/ppermute | solution.py:24
  118.5 0.0 copy-done.1
  118.5 14.8 %shard_map.141 = (f32[128,128]{1,0:T(8,128)}, f32[256,128]{1,0:T(8,128)S(1)}) custom-call(s32[2]{0:T(128)S(1)} %copy-done.1, f32[256,128]{1,0:T(8,128)S(1)} %get-tuple-element.17.own_ref, f32[256,128]{1,0:T(8,128)S(1)} %collective-permute-done.11.partner_ref, f32[256,128]{1,0:T(8,128)S(1)} %constant_dynamic-update-slice_fusion.sketch_ref), custom_call_target="tpu_custom_call" | custom-call | tf_op jit(solution)/shard_map/pallas_call | solution.py:201
  133.3 0.6 constant_dynamic-slice_fusion
  (15 shorter events, 0.3 us)
Async XLA Ops:
  26.2 2.9 %collective-permute-start = (bf16[4,8,64,256]{3,2,1,0:T(8,128)(2,1)}, bf16[4,8,64,256]{3,2,1,0:T(8,128)(2,1)S(1)}, u32[]{:S(2)}, u32[]{:S(2)}) collective-permute-start(bf16[4,8,64,256]{3,2,1,0:T(8,128)(2,1)} %get-tuple-element.13), channel_id=1, source_target_pairs={{0,4},{4,0},{8,12},{12,8},{16,20},{20,16},{24,28},{28,24},{1,5},{5... | collective-permute-start | bytes 3145736 | tf_op jit(solution)/shard_map/ppermute | solution.py:24
  31.0 3.3 %copy-start.2 = (f32[64,128]{1,0:T(8,128)S(1)}, f32[64,128]{1,0:T(8,128)}, u32[]{:S(2)}) copy-start(f32[64,128]{1,0:T(8,128)} %param.18) | copy-start | bytes 98308
  31.3 10.1 %collective-permute-start.3 = (bf16[2,4,64,256]{3,2,1,0:T(8,128)(2,1)S(1)}, bf16[2,4,64,256]{3,2,1,0:T(8,128)(2,1)S(1)}, u32[]{:S(2)}, u32[]{:S(2)}) collective-permute-start(bf16[2,4,64,256]{3,2,1,0:T(8,128)(2,1)S(1)} %fusion.1), channel_id=1, source_target_pairs={{0,16},{4,20},{8,24},{12,28},{16,0},{20,4},{24,8},{28,12},{1,17},{... | collective-permute-start | bytes 786440 | tf_op jit(solution)/shard_map/ppermute | solution.py:24
  34.3 23.8 %collective-permute-start.5 = (f32[64,128]{1,0:T(8,128)S(1)}, f32[64,128]{1,0:T(8,128)S(1)}, u32[]{:S(2)}, u32[]{:S(2)}) collective-permute-start(f32[64,128]{1,0:T(8,128)S(1)} %copy-done.2), channel_id=1, source_target_pairs={{0,1},{1,2},{2,3},{3,0},{4,5},{5,6},{6,7},{7,4},{8,9},{9,10},{10,1... | collective-permute-start | bytes 98312 | tf_op jit(solution)/shard_map/ppermute | solution.py:34
  35.8 22.3 %collective-permute-start.6 = (f32[64,128]{1,0:T(8,128)S(1)}, f32[64,128]{1,0:T(8,128)S(1)}, u32[]{:S(2)}, u32[]{:S(2)}) collective-permute-start(f32[64,128]{1,0:T(8,128)S(1)} %copy-done.2), channel_id=1, source_target_pairs={{0,2},{1,3},{2,0},{3,1},{4,6},{5,7},{6,4},{7,5},{8,10},{9,11},{10,... | collective-permute-start | bytes 98312 | tf_op jit(solution)/shard_map/ppermute | solution.py:34
  38.4 19.7 %collective-permute-start.7 = (f32[64,128]{1,0:T(8,128)S(1)}, f32[64,128]{1,0:T(8,128)S(1)}, u32[]{:S(2)}, u32[]{:S(2)}) collective-permute-start(f32[64,128]{1,0:T(8,128)S(1)} %copy-done.2), channel_id=1, source_target_pairs={{0,3},{1,0},{2,1},{3,2},{4,7},{5,4},{6,5},{7,6},{8,11},{9,8},{10,9... | collective-permute-start | bytes 98312 | tf_op jit(solution)/shard_map/ppermute | solution.py:34
  39.8 8.7 %collective-permute-start.1 = (bf16[2,4,64,256]{3,2,1,0:T(8,128)(2,1)S(1)}, bf16[2,4,64,256]{3,2,1,0:T(8,128)(2,1)S(1)}, u32[]{:S(2)}, u32[]{:S(2)}) collective-permute-start(bf16[2,4,64,256]{3,2,1,0:T(8,128)(2,1)S(1)} %fusion), channel_id=1, source_target_pairs={{0,8},{4,12},{8,0},{12,4},{16,24},{20,28},{24,16},{28,20},{1,9},{5... | collective-permute-start | bytes 786440 | tf_op jit(solution)/shard_map/ppermute | solution.py:24
  41.5 8.4 %collective-permute-start.4 = (bf16[4,64,256]{2,1,0:T(8,128)(2,1)S(1)}, bf16[4,64,256]{2,1,0:T(8,128)(2,1)S(1)}, u32[]{:S(2)}, u32[]{:S(2)}) collective-permute-start(bf16[4,64,256]{2,1,0:T(8,128)(2,1)S(1)} %fusion.5), channel_id=1, source_target_pairs={{0,8},{4,12},{8,0},{12,4},{16,24},{20,28},{24,16},{28,20},{1,9},{5... | collective-permute-start | bytes 393224 | tf_op jit(solution)/shard_map/ppermute | solution.py:24
  48.6 5.0 %collective-permute-start.2 = (bf16[4,64,256]{2,1,0:T(8,128)(2,1)S(1)}, bf16[4,64,256]{2,1,0:T(8,128)(2,1)S(1)}, u32[]{:S(2)}, u32[]{:S(2)}) collective-permute-start(bf16[4,64,256]{2,1,0:T(8,128)(2,1)S(1)} %fusion.4), channel_id=1, source_target_pairs={{0,16},{4,20},{8,24},{12,28},{16,0},{20,4},{24,8},{28,12},{1,17},{... | collective-permute-start | bytes 393224 | tf_op jit(solution)/shard_map/ppermute | solution.py:24
  54.4 10.2 %all-to-all-start = ((bf16[4,2,64,256]{3,2,1,0:T(8,128)(2,1)}), bf16[4,2,64,256]{3,2,1,0:T(8,128)(2,1)S(1)}, u32[]{:S(2)}, u32[]{:S(2)}) async-start(bf16[4,2,64,256]{3,2,1,0:T(8,128)(2,1)} %bitcast.11), calls=%async_computation | async-start | bytes 524288 | tf_op jit(solution)/shard_map/all_to_all | solution.py:257
  65.0 33.1 %copy-start = (s32[4]{0:T(128)S(1)}, s32[4]{0:T(128)}, u32[]{:S(2)}) copy-start(s32[4]{0:T(128)} %rank_ref.3) | copy-start | bytes 52
  65.0 53.5 %copy-start.1 = (s32[2]{0:T(128)S(1)}, s32[2]{0:T(128)}, u32[]{:S(2)}) copy-start(s32[2]{0:T(128)} %rank_ref.4) | copy-start | bytes 28
  66.5 8.1 %collective-permute-start.8 = (f32[384,128]{1,0:T(8,128)S(1)}, f32[384,128]{1,0:T(8,128)S(1)}, u32[]{:S(2)}, u32[]{:S(2)}) collective-permute-start(f32[384,128]{1,0:T(8,128)S(1)} %pad_maximum_fusion.1), channel_id=1, source_target_pairs={{0,1},{1,0},{2,3},{3,2},{4,5},{5,4},{6,7},{7,6},{8,9},{9,8},{10,11... | collective-permute-start | bytes 589832 | tf_op jit(solution)/shard_map/ppermute | solution.py:24
  74.6 8.5 %collective-permute-start.9 = (f32[384,128]{1,0:T(8,128)S(1)}, f32[384,128]{1,0:T(8,128)S(1)}, u32[]{:S(2)}, u32[]{:S(2)}) collective-permute-start(f32[384,128]{1,0:T(8,128)S(1)} %fusion.6), channel_id=1, source_target_pairs={{0,2},{1,3},{2,0},{3,1},{4,6},{5,7},{6,4},{7,5},{8,10},{9,11},{10,... | collective-permute-start | bytes 589832 | tf_op jit(solution)/shard_map/ppermute | solution.py:24
  96.7 1.3 %collective-permute-start.10 = (f32[256,128]{1,0:T(8,128)S(1)}, f32[256,128]{1,0:T(8,128)S(1)}, u32[]{:S(2)}, u32[]{:S(2)}) collective-permute-start(f32[256,128]{1,0:T(8,128)S(1)} %get-tuple-element.15.own_ref), channel_id=1, source_target_pairs={{0,4},{4,0},{8,12},{12,8},{16,20},{20,16},{24,28},{28,24},{1,5},{5... | collective-permute-start | bytes 393224 | tf_op jit(solution)/shard_map/ppermute | solution.py:24
  112.9 5.5 %collective-permute-start.11 = (f32[256,128]{1,0:T(8,128)S(1)}, f32[256,128]{1,0:T(8,128)S(1)}, u32[]{:S(2)}, u32[]{:S(2)}) collective-permute-start(f32[256,128]{1,0:T(8,128)S(1)} %get-tuple-element.17.own_ref), channel_id=1, source_target_pairs={{0,8},{4,12},{8,0},{12,4},{16,24},{20,28},{24,16},{28,20},{1,9},{5... | collective-permute-start | bytes 393224 | tf_op jit(solution)/shard_map/ppermute | solution.py:24

commit v3 on v2

--- a/solution.py
+++ b/solution.py
@@ -8,7 +8,7 @@
 
 highest = lax.Precision.HIGHEST
 WIDE = 256
-PANEL = 16
+PANEL = 32
 KIDS = 2
 
 

time: 135 us -> 132 us (0.978)
  Pallas kernels: 67.4 us -> 64.5 us
    pallas_call x3, Pallas kernels: 43.3 us -> 40.4 us  [basis_call(): pl.pallas_call(kernel, in_specs=[pl.BlockSpec(memory_space=pltpu.SMEM)] +...]
where the time goes in v3:
time: 132 us; the launch traced here: 131 us
  Pallas kernels  64.5 us (49%)
  waiting for transfers between devices  36.9 us (28%)
  starting transfers between devices  21.1 us (16%)
  other arithmetic  2.86 us (2%)
  local copies, waits for them, and re-layouts  2.74 us (2%)
  between operations  1.54 us (1%)
  matrix products  1.45 us (1%)
    pallas_call x3, Pallas kernels, basis_call(): pl.pallas_call(kernel, in_specs=[pl.BlockSpec(memory_space=pltpu.SMEM)] +...  40.4 us
    ppermute x9, waiting for transfers between devices, partner_of(): return lax.ppermute(block, axis, route)  30.4 us
    pallas_call x1, Pallas kernels, local_samples(): pl.pallas_call(sample_kernel, grid_spec=grid_spec, out_shape=[jax.ShapeDt...  24.1 us
    ppermute x9, starting transfers between devices, partner_of(): return lax.ppermute(block, axis, route)  12 us
    all_to_all x1, waiting for transfers between devices, on_device(): share = lax.all_to_all(share, 'probe', 0, 0, tiled=True)  6.48 us
    ppermute x3, starting transfers between devices, gathered(): lax.ppermute(block, axis, [(i, (i + shift) % count) for i in range(count)])  5.51 us
    all_to_all x1, starting transfers between devices, on_device(): share = lax.all_to_all(share, 'probe', 0, 0, tiled=True)  3.59 us
  transfers between devices with their start and end apart: 13, of which 9 were waited for; matrix products, arithmetic and copies ran while one was open for 1% of the time, Pallas kernels for 0%

profile of v3, /device:TPU:0, one launch (start us, length us, event | category | flops | bytes accessed | tf_op | source)
XLA Modules:
  0.0 131.1 jit_solution(16182914682311025001)
XLA Ops:
  0.6 0.8 copy.19
  1.4 0.7 reshape.31.coup_ref
  2.1 24.1 %shard_map.138 = (bf16[4,8,64,256]{3,2,1,0:T(8,128)(2,1)}, f32[4,8,64,256]{3,2,1,0:T(8,128)}) custom-call(s32[128]{0:T(128)} %bitcast.40, s32[128]{0:T(128)} %reshape.31.coup_ref, bf16[32,512,512]{2,1,0:T(8,128)(2,1)} %upd_ref.1, bf16[64,16384]{1,0:T(8,128)(2,1)} %probe_ref.1, s32[32,4,128]{2,1,0:T(4,128)} %bitcast.39, bf16[64,128,128]{2,1,0:T(8,128)(2,1)} %blk_ref.1, ...), custom_call_target="tpu_custom_call" | custom-call | tf_op jit(solution)/shard_map/pallas_call | solution.py:118
  26.2 0.4 collective-permute-start
  26.6 2.5 %collective-permute-done = bf16[4,8,64,256]{3,2,1,0:T(8,128)(2,1)S(1)} collective-permute-done((bf16[4,8,64,256]{3,2,1,0:T(8,128)(2,1)}, bf16[4,8,64,256]{3,2,1,0:T(8,128)(2,1)S(1)}, u32[]{:S(2)}, u32[]{:S(2)}) %collective-permute-start) | collective-permute-done | bytes 1048608 | tf_op jit(solution)/shard_map/ppermute | solution.py:24
  29.1 1.9 %convert_add_fusion = f32[4,8,64,256]{3,2,1,0:T(8,128)S(1)} fusion(f32[4,8,64,256]{3,2,1,0:T(8,128)} %get-tuple-element.12, bf16[4,8,64,256]{3,2,1,0:T(8,128)(2,1)S(1)} %collective-permute-done), kind=kLoop, calls=%fused_computation | loop fusion | flops 1048576 | bytes 5242880 | tf_op jit(solution)/shard_map/add | solution.py:247
  31.0 0.0 copy-start.2
  31.0 0.2 fusion.7
  31.3 2.9 %collective-permute-start.3 = (bf16[2,4,64,256]{3,2,1,0:T(8,128)(2,1)S(1)}, bf16[2,4,64,256]{3,2,1,0:T(8,128)(2,1)S(1)}, u32[]{:S(2)}, u32[]{:S(2)}) collective-permute-start(bf16[2,4,64,256]{3,2,1,0:T(8,128)(2,1)S(1)} %fusion.1), channel_id=1, source_target_pairs={{0,16},{4,20},{8,24},{12,28},{16,0},{20,4},{24,8},{28,12},{1,17},{... | collective-permute-start | bytes 786440 | tf_op jit(solution)/shard_map/ppermute | solution.py:24
  34.2 0.0 copy-done.2
  34.2 1.6 %collective-permute-start.5 = (f32[64,128]{1,0:T(8,128)S(1)}, f32[64,128]{1,0:T(8,128)S(1)}, u32[]{:S(2)}, u32[]{:S(2)}) collective-permute-start(f32[64,128]{1,0:T(8,128)S(1)} %copy-done.2), channel_id=1, source_target_pairs={{0,1},{1,2},{2,3},{3,0},{4,5},{5,6},{6,7},{7,4},{8,9},{9,10},{10,1... | collective-permute-start | bytes 98312 | tf_op jit(solution)/shard_map/ppermute | solution.py:34
  35.8 2.6 %collective-permute-start.6 = (f32[64,128]{1,0:T(8,128)S(1)}, f32[64,128]{1,0:T(8,128)S(1)}, u32[]{:S(2)}, u32[]{:S(2)}) collective-permute-start(f32[64,128]{1,0:T(8,128)S(1)} %copy-done.2), channel_id=1, source_target_pairs={{0,2},{1,3},{2,0},{3,1},{4,6},{5,7},{6,4},{7,5},{8,10},{9,11},{10,... | collective-permute-start | bytes 98312 | tf_op jit(solution)/shard_map/ppermute | solution.py:34
  38.4 1.3 %collective-permute-start.7 = (f32[64,128]{1,0:T(8,128)S(1)}, f32[64,128]{1,0:T(8,128)S(1)}, u32[]{:S(2)}, u32[]{:S(2)}) collective-permute-start(f32[64,128]{1,0:T(8,128)S(1)} %copy-done.2), channel_id=1, source_target_pairs={{0,3},{1,0},{2,1},{3,2},{4,7},{5,4},{6,5},{7,6},{8,11},{9,8},{10,9... | collective-permute-start | bytes 98312 | tf_op jit(solution)/shard_map/ppermute | solution.py:34
  39.8 1.6 %collective-permute-start.1 = (bf16[2,4,64,256]{3,2,1,0:T(8,128)(2,1)S(1)}, bf16[2,4,64,256]{3,2,1,0:T(8,128)(2,1)S(1)}, u32[]{:S(2)}, u32[]{:S(2)}) collective-permute-start(bf16[2,4,64,256]{3,2,1,0:T(8,128)(2,1)S(1)} %fusion), channel_id=1, source_target_pairs={{0,8},{4,12},{8,0},{12,4},{16,24},{20,28},{24,16},{28,20},{1,9},{5... | collective-permute-start | bytes 786440 | tf_op jit(solution)/shard_map/ppermute | solution.py:24
  41.4 0.0 collective-permute-done.3
  41.4 0.1 bitcast_add_fusion
  41.5 1.3 collective-permute-start.4
  42.7 5.8 %collective-permute-done.1 = bf16[2,4,64,256]{3,2,1,0:T(8,128)(2,1)S(1)} collective-permute-done((bf16[2,4,64,256]{3,2,1,0:T(8,128)(2,1)S(1)}, bf16[2,4,64,256]{3,2,1,0:T(8,128)(2,1)S(1)}, u32[]{:S(2)}, u32[]{:S(2)}) %collective-permute-start.1) | collective-permute-done | bytes 262176 | tf_op jit(solution)/shard_map/ppermute | solution.py:24
  48.5 0.1 bitcast_add_fusion.1
  48.6 0.8 collective-permute-start.2
  49.3 0.5 collective-permute-done.4
  49.9 3.7 %collective-permute-done.2 = bf16[4,64,256]{2,1,0:T(8,128)(2,1)S(1)} collective-permute-done((bf16[4,64,256]{2,1,0:T(8,128)(2,1)S(1)}, bf16[4,64,256]{2,1,0:T(8,128)(2,1)S(1)}, u32[]{:S(2)}, u32[]{:S(2)}) %collective-permute-start.2) | collective-permute-done | bytes 131104 | tf_op jit(solution)/shard_map/ppermute | solution.py:24
  53.7 0.7 pad_maximum_fusion
  54.4 3.6 %all-to-all-start = ((bf16[4,2,64,256]{3,2,1,0:T(8,128)(2,1)}), bf16[4,2,64,256]{3,2,1,0:T(8,128)(2,1)S(1)}, u32[]{:S(2)}, u32[]{:S(2)}) async-start(bf16[4,2,64,256]{3,2,1,0:T(8,128)(2,1)} %bitcast.11), calls=%async_computation | async-start | bytes 524288 | tf_op jit(solution)/shard_map/all_to_all | solution.py:257
  58.1 0.0 collective-permute-done.5
  58.1 0.0 collective-permute-done.6
  58.1 0.0 collective-permute-done.7
  58.1 6.5 %all-to-all-done = bf16[4,2,64,256]{3,2,1,0:T(8,128)(2,1)S(1)} async-done(((bf16[4,2,64,256]{3,2,1,0:T(8,128)(2,1)}), bf16[4,2,64,256]{3,2,1,0:T(8,128)(2,1)S(1)}, u32[]{:S(2)}, u32[]{:S(2)}) %all-to-all-start) | async-done | bytes 262176 | tf_op jit(solution)/shard_map/all_to_all | solution.py:257
  64.6 0.3 copy.20
  64.9 0.0 copy-start
  65.0 0.0 copy-start.1
  65.0 0.5 fusion.8.sketched_ref
  65.4 0.4 fusion.10
  65.8 0.6 fusion.9
  66.4 2.8 %collective-permute-start.8 = (f32[384,128]{1,0:T(8,128)S(1)}, f32[384,128]{1,0:T(8,128)S(1)}, u32[]{:S(2)}, u32[]{:S(2)}) collective-permute-start(f32[384,128]{1,0:T(8,128)S(1)} %pad_maximum_fusion.1), channel_id=1, source_target_pairs={{0,1},{1,0},{2,3},{3,2},{4,5},{5,4},{6,7},{7,6},{8,9},{9,8},{10,11... | collective-permute-start | bytes 589832 | tf_op jit(solution)/shard_map/ppermute | solution.py:24
  69.2 5.3 %collective-permute-done.8 = f32[384,128]{1,0:T(8,128)S(1)} collective-permute-done((f32[384,128]{1,0:T(8,128)S(1)}, f32[384,128]{1,0:T(8,128)S(1)}, u32[]{:S(2)}, u32[]{:S(2)}) %collective-permute-start.8) | collective-permute-done | bytes 196640 | tf_op jit(solution)/shard_map/ppermute | solution.py:24
  74.6 0.7 collective-permute-start.9
  75.9 7.2 %collective-permute-done.9 = f32[384,128]{1,0:T(8,128)S(1)} collective-permute-done((f32[384,128]{1,0:T(8,128)S(1)}, f32[384,128]{1,0:T(8,128)S(1)}, u32[]{:S(2)}, u32[]{:S(2)}) %collective-permute-start.9) | collective-permute-done | bytes 196640 | tf_op jit(solution)/shard_map/ppermute | solution.py:24
  83.1 12.6 %shard_map.139 = (f32[512,128]{1,0:T(8,128)}, f32[256,128]{1,0:T(8,128)S(1)}) custom-call(s32[1]{0:T(128)S(6)} %copy.26.rank_ref, f32[384,128]{1,0:T(8,128)S(1)} %add.115.sums_ref, f32[512,128]{1,0:T(8,128)S(1)} %fusion.8.sketched_ref), custom_call_target="tpu_custom_call" | custom-call | tf_op jit(solution)/shard_map/pallas_call | solution.py:201
  95.8 0.0 collective-permute-start.10
  95.8 1.3 %collective-permute-done.10.partner_ref = f32[256,128]{1,0:T(8,128)S(1)} collective-permute-done((f32[256,128]{1,0:T(8,128)S(1)}, f32[256,128]{1,0:T(8,128)S(1)}, u32[]{:S(2)}, u32[]{:S(2)}) %collective-permute-start.10) | collective-permute-done | bytes 131104 | tf_op jit(solution)/shard_map/ppermute | solution.py:24
  97.1 0.0 copy-done
  97.1 13.9 %shard_map.140 = (f32[128,128]{1,0:T(8,128)}, f32[256,128]{1,0:T(8,128)S(1)}) custom-call(s32[4]{0:T(128)S(1)} %copy-done, f32[256,128]{1,0:T(8,128)S(1)} %get-tuple-element.15.own_ref, f32[256,128]{1,0:T(8,128)S(1)} %collective-permute-done.10.partner_ref, f32[256,128]{1,0:T(8,128)S(1)} %constant_dynamic-update-slice_fusion.sketch_ref), custom_call_target="tpu_custom_call" | custom-call | tf_op jit(solution)/shard_map/pallas_call | solution.py:201
  111.0 1.5 %collective-permute-start.11 = (f32[256,128]{1,0:T(8,128)S(1)}, f32[256,128]{1,0:T(8,128)S(1)}, u32[]{:S(2)}, u32[]{:S(2)}) collective-permute-start(f32[256,128]{1,0:T(8,128)S(1)} %get-tuple-element.17.own_ref), channel_id=1, source_target_pairs={{0,8},{4,12},{8,0},{12,4},{16,24},{20,28},{24,16},{28,20},{1,9},{5... | collective-permute-start | bytes 393224 | tf_op jit(solution)/shard_map/ppermute | solution.py:24
  112.5 4.0 %collective-permute-done.11.partner_ref = f32[256,128]{1,0:T(8,128)S(1)} collective-permute-done((f32[256,128]{1,0:T(8,128)S(1)}, f32[256,128]{1,0:T(8,128)S(1)}, u32[]{:S(2)}, u32[]{:S(2)}) %collective-permute-start.11) | collective-permute-done | bytes 131104 | tf_op jit(solution)/shard_map/ppermute | solution.py:24
  116.6 0.0 copy-done.1
  116.6 13.9 %shard_map.141 = (f32[128,128]{1,0:T(8,128)}, f32[256,128]{1,0:T(8,128)S(1)}) custom-call(s32[2]{0:T(128)S(1)} %copy-done.1, f32[256,128]{1,0:T(8,128)S(1)} %get-tuple-element.17.own_ref, f32[256,128]{1,0:T(8,128)S(1)} %collective-permute-done.11.partner_ref, f32[256,128]{1,0:T(8,128)S(1)} %constant_dynamic-update-slice_fusion.sketch_ref), custom_call_target="tpu_custom_call" | custom-call | tf_op jit(solution)/shard_map/pallas_call | solution.py:201
  130.5 0.6 constant_dynamic-slice_fusion
  (15 shorter events, 0.3 us)
Async XLA Ops:
  26.2 2.9 %collective-permute-start = (bf16[4,8,64,256]{3,2,1,0:T(8,128)(2,1)}, bf16[4,8,64,256]{3,2,1,0:T(8,128)(2,1)S(1)}, u32[]{:S(2)}, u32[]{:S(2)}) collective-permute-start(bf16[4,8,64,256]{3,2,1,0:T(8,128)(2,1)} %get-tuple-element.13), channel_id=1, source_target_pairs={{0,4},{4,0},{8,12},{12,8},{16,20},{20,16},{24,28},{28,24},{1,5},{5... | collective-permute-start | bytes 3145736 | tf_op jit(solution)/shard_map/ppermute | solution.py:24
  31.0 3.2 %copy-start.2 = (f32[64,128]{1,0:T(8,128)S(1)}, f32[64,128]{1,0:T(8,128)}, u32[]{:S(2)}) copy-start(f32[64,128]{1,0:T(8,128)} %param.18) | copy-start | bytes 98308
  31.3 10.1 %collective-permute-start.3 = (bf16[2,4,64,256]{3,2,1,0:T(8,128)(2,1)S(1)}, bf16[2,4,64,256]{3,2,1,0:T(8,128)(2,1)S(1)}, u32[]{:S(2)}, u32[]{:S(2)}) collective-permute-start(bf16[2,4,64,256]{3,2,1,0:T(8,128)(2,1)S(1)} %fusion.1), channel_id=1, source_target_pairs={{0,16},{4,20},{8,24},{12,28},{16,0},{20,4},{24,8},{28,12},{1,17},{... | collective-permute-start | bytes 786440 | tf_op jit(solution)/shard_map/ppermute | solution.py:24
  34.2 23.8 %collective-permute-start.5 = (f32[64,128]{1,0:T(8,128)S(1)}, f32[64,128]{1,0:T(8,128)S(1)}, u32[]{:S(2)}, u32[]{:S(2)}) collective-permute-start(f32[64,128]{1,0:T(8,128)S(1)} %copy-done.2), channel_id=1, source_target_pairs={{0,1},{1,2},{2,3},{3,0},{4,5},{5,6},{6,7},{7,4},{8,9},{9,10},{10,1... | collective-permute-start | bytes 98312 | tf_op jit(solution)/shard_map/ppermute | solution.py:34
  35.8 22.3 %collective-permute-start.6 = (f32[64,128]{1,0:T(8,128)S(1)}, f32[64,128]{1,0:T(8,128)S(1)}, u32[]{:S(2)}, u32[]{:S(2)}) collective-permute-start(f32[64,128]{1,0:T(8,128)S(1)} %copy-done.2), channel_id=1, source_target_pairs={{0,2},{1,3},{2,0},{3,1},{4,6},{5,7},{6,4},{7,5},{8,10},{9,11},{10,... | collective-permute-start | bytes 98312 | tf_op jit(solution)/shard_map/ppermute | solution.py:34
  38.4 19.7 %collective-permute-start.7 = (f32[64,128]{1,0:T(8,128)S(1)}, f32[64,128]{1,0:T(8,128)S(1)}, u32[]{:S(2)}, u32[]{:S(2)}) collective-permute-start(f32[64,128]{1,0:T(8,128)S(1)} %copy-done.2), channel_id=1, source_target_pairs={{0,3},{1,0},{2,1},{3,2},{4,7},{5,4},{6,5},{7,6},{8,11},{9,8},{10,9... | collective-permute-start | bytes 98312 | tf_op jit(solution)/shard_map/ppermute | solution.py:34
  39.8 8.7 %collective-permute-start.1 = (bf16[2,4,64,256]{3,2,1,0:T(8,128)(2,1)S(1)}, bf16[2,4,64,256]{3,2,1,0:T(8,128)(2,1)S(1)}, u32[]{:S(2)}, u32[]{:S(2)}) collective-permute-start(bf16[2,4,64,256]{3,2,1,0:T(8,128)(2,1)S(1)} %fusion), channel_id=1, source_target_pairs={{0,8},{4,12},{8,0},{12,4},{16,24},{20,28},{24,16},{28,20},{1,9},{5... | collective-permute-start | bytes 786440 | tf_op jit(solution)/shard_map/ppermute | solution.py:24
  41.5 8.4 %collective-permute-start.4 = (bf16[4,64,256]{2,1,0:T(8,128)(2,1)S(1)}, bf16[4,64,256]{2,1,0:T(8,128)(2,1)S(1)}, u32[]{:S(2)}, u32[]{:S(2)}) collective-permute-start(bf16[4,64,256]{2,1,0:T(8,128)(2,1)S(1)} %fusion.5), channel_id=1, source_target_pairs={{0,8},{4,12},{8,0},{12,4},{16,24},{20,28},{24,16},{28,20},{1,9},{5... | collective-permute-start | bytes 393224 | tf_op jit(solution)/shard_map/ppermute | solution.py:24
  48.6 5.0 %collective-permute-start.2 = (bf16[4,64,256]{2,1,0:T(8,128)(2,1)S(1)}, bf16[4,64,256]{2,1,0:T(8,128)(2,1)S(1)}, u32[]{:S(2)}, u32[]{:S(2)}) collective-permute-start(bf16[4,64,256]{2,1,0:T(8,128)(2,1)S(1)} %fusion.4), channel_id=1, source_target_pairs={{0,16},{4,20},{8,24},{12,28},{16,0},{20,4},{24,8},{28,12},{1,17},{... | collective-permute-start | bytes 393224 | tf_op jit(solution)/shard_map/ppermute | solution.py:24
  54.4 10.2 %all-to-all-start = ((bf16[4,2,64,256]{3,2,1,0:T(8,128)(2,1)}), bf16[4,2,64,256]{3,2,1,0:T(8,128)(2,1)S(1)}, u32[]{:S(2)}, u32[]{:S(2)}) async-start(bf16[4,2,64,256]{3,2,1,0:T(8,128)(2,1)} %bitcast.11), calls=%async_computation | async-start | bytes 524288 | tf_op jit(solution)/shard_map/all_to_all | solution.py:257
  64.9 32.2 %copy-start = (s32[4]{0:T(128)S(1)}, s32[4]{0:T(128)}, u32[]{:S(2)}) copy-start(s32[4]{0:T(128)} %rank_ref.3) | copy-start | bytes 52
  65.0 51.6 %copy-start.1 = (s32[2]{0:T(128)S(1)}, s32[2]{0:T(128)}, u32[]{:S(2)}) copy-start(s32[2]{0:T(128)} %rank_ref.4) | copy-start | bytes 28
  66.4 8.1 %collective-permute-start.8 = (f32[384,128]{1,0:T(8,128)S(1)}, f32[384,128]{1,0:T(8,128)S(1)}, u32[]{:S(2)}, u32[]{:S(2)}) collective-permute-start(f32[384,128]{1,0:T(8,128)S(1)} %pad_maximum_fusion.1), channel_id=1, source_target_pairs={{0,1},{1,0},{2,3},{3,2},{4,5},{5,4},{6,7},{7,6},{8,9},{9,8},{10,11... | collective-permute-start | bytes 589832 | tf_op jit(solution)/shard_map/ppermute | solution.py:24
  74.6 8.6 %collective-permute-start.9 = (f32[384,128]{1,0:T(8,128)S(1)}, f32[384,128]{1,0:T(8,128)S(1)}, u32[]{:S(2)}, u32[]{:S(2)}) collective-permute-start(f32[384,128]{1,0:T(8,128)S(1)} %fusion.6), channel_id=1, source_target_pairs={{0,2},{1,3},{2,0},{3,1},{4,6},{5,7},{6,4},{7,5},{8,10},{9,11},{10,... | collective-permute-start | bytes 589832 | tf_op jit(solution)/shard_map/ppermute | solution.py:24
  95.8 1.3 %collective-permute-start.10 = (f32[256,128]{1,0:T(8,128)S(1)}, f32[256,128]{1,0:T(8,128)S(1)}, u32[]{:S(2)}, u32[]{:S(2)}) collective-permute-start(f32[256,128]{1,0:T(8,128)S(1)} %get-tuple-element.15.own_ref), channel_id=1, source_target_pairs={{0,4},{4,0},{8,12},{12,8},{16,20},{20,16},{24,28},{28,24},{1,5},{5... | collective-permute-start | bytes 393224 | tf_op jit(solution)/shard_map/ppermute | solution.py:24
  111.0 5.5 %collective-permute-start.11 = (f32[256,128]{1,0:T(8,128)S(1)}, f32[256,128]{1,0:T(8,128)S(1)}, u32[]{:S(2)}, u32[]{:S(2)}) collective-permute-start(f32[256,128]{1,0:T(8,128)S(1)} %get-tuple-element.17.own_ref), channel_id=1, source_target_pairs={{0,8},{4,12},{8,0},{12,4},{16,24},{20,28},{24,16},{28,20},{1,9},{5... | collective-permute-start | bytes 393224 | tf_op jit(solution)/shard_map/ppermute | solution.py:24

commit v4 on v3

--- a/solution.py
+++ b/solution.py
@@ -123,6 +123,9 @@
             jax.ShapeDtypeStruct((half, high, probes, WIDE), jnp.float32),
         ],
         compiler_params=pltpu.CompilerParams(vmem_limit_bytes=56 * 1024 * 1024),
+        cost_estimate=pl.CostEstimate(
+            flops=20 * 10**9, bytes_accessed=child_updates.size * 2, transcendentals=0
+        ),
     )(child_dest.reshape(-1), coupling.reshape(-1), child_updates, child_probes, rows,
       parent_blocks, parent_probes)
 
@@ -171,10 +174,9 @@
     return jnp.where(columns < rank, result, 0.0)
 
 
-def front_kernel(rank_ref, sums_ref, sketched_ref, basis_ref, passed_ref, work_u, work_v, done):
-    n = done.shape[0]
-    inverse = inverse_factor(work_u, work_v, done, sums_ref[:n])
-    passed_ref[...] = limited(sums_ref[n:], inverse, rank_ref[0])
+def front_kernel(rank_ref, gram_ref, sketched_ref, basis_ref, inverse_ref, work_u, work_v, done):
+    inverse = inverse_factor(work_u, work_v, done, gram_ref[...])
+    inverse_ref[...] = inverse
     basis_ref[...] = limited(sketched_ref[...], inverse, rank_ref[0])
 
 
@@ -206,6 +208,7 @@
         out_shape=[jax.ShapeDtypeStruct(shape, jnp.float32) for shape in outs],
         scratch_shapes=[pltpu.VMEM((n, n), jnp.float32)] * 3,
         compiler_params=pltpu.CompilerParams(vmem_limit_bytes=24 * 1024 * 1024),
+        cost_estimate=pl.CostEstimate(flops=12 * 10**9, bytes_accessed=2**19, transcendentals=n),
     )(*operands)
 
 
@@ -260,14 +263,16 @@
     sketched = jnp.einsum("pr,ps->rs", rows_mine, sketch_all, precision=highest)
     gram = jnp.einsum("ra,rb->ab", sketched, sketched, precision=highest)
     crossed = jnp.dot(rows_mine, sketched, precision=highest)
-    sums = jnp.concatenate([gram, crossed], 0)
     stride = 0
     while 1 << stride < probe_count:
-        sums = sums + partner_of(sums, "probe", stride)
+        gram = gram + partner_of(gram, "probe", stride)
+        crossed = crossed + partner_of(crossed, "probe", stride)
         stride += 1
-    own_basis, passed_one = basis_call(
-        front_kernel, [sketched.shape, crossed.shape], rank_width, rank_one, sums, sketched
-    )
+    own_basis, inverse = basis_call(
+        front_kernel, [sketched.shape, gram.shape], rank_width, rank_one, gram, sketched
+    )
+    passed_one = jnp.einsum("pr,sr->ps", crossed, inverse, precision=highest)
+    passed_one = jnp.where(jnp.arange(rank_width)[None, :] < rank_one[0], passed_one, 0.0)
     basis_two, passed_two = merge(passed_one, 0, sketch_all, rank_two)
     basis_three, passed_three = merge(passed_two, 1, sketch_all, rank_three)
     top = lax.dynamic_slice_in_dim(passed_three, probe_index * probes, probes, 0)

time: 132 us -> 126 us (0.955)
  waiting for transfers between devices: 36.9 us -> 29.9 us
    ppermute x9 -> x11, waiting for transfers between devices: 30.4 us -> 23.4 us  [partner_of(): return lax.ppermute(block, axis, route)]
    ppermute x9 -> x11, starting transfers between devices: 12 us -> 12.5 us  [partner_of(): return lax.ppermute(block, axis, route)]
  transfers between devices with their start and end apart: 13 -> 15, of which waited for: 9 -> 10; matrix products, arithmetic and copies ran while one was open for 1% -> 1% of each run, Pallas kernels for 0% -> 10%
where the time goes in v4:
time: 126 us; the launch traced here: 125 us
  Pallas kernels  64.4 us (51%)
  waiting for transfers between devices  29.9 us (24%)
  starting transfers between devices  21.6 us (17%)
  other arithmetic  2.84 us (2%)
  local copies, waits for them, and re-layouts  2.74 us (2%)
  matrix products  1.71 us (1%)
  between operations  1.55 us (1%)
    pallas_call x3, Pallas kernels, basis_call(): pl.pallas_call(kernel, in_specs=[pl.BlockSpec(memory_space=pltpu.SMEM)] +...  40.3 us
    pallas_call x1, Pallas kernels, local_samples(): pl.pallas_call(sample_kernel, grid_spec=grid_spec, out_shape=[jax.ShapeDt...  24.1 us
    ppermute x11, waiting for transfers between devices, partner_of(): return lax.ppermute(block, axis, route)  23.4 us
    ppermute x11, starting transfers between devices, partner_of(): return lax.ppermute(block, axis, route)  12.5 us
    all_to_all x1, waiting for transfers between devices, on_device(): share = lax.all_to_all(share, 'probe', 0, 0, tiled=True)  6.5 us
    ppermute x3, starting transfers between devices, gathered(): lax.ppermute(block, axis, [(i, (i + shift) % count) for i in range(count)])  5.51 us
    all_to_all x1, starting transfers between devices, on_device(): share = lax.all_to_all(share, 'probe', 0, 0, tiled=True)  3.59 us
  transfers between devices with their start and end apart: 15, of which 10 were waited for; matrix products, arithmetic and copies ran while one was open for 1% of the time, Pallas kernels for 10%

profile of v4, /device:TPU:0, one launch (start us, length us, event | category | flops | bytes accessed | tf_op | source)
XLA Modules:
  0.0 124.8 jit_solution(9432698078259483074)
XLA Ops:
  0.6 0.8 copy.19
  1.4 0.7 reshape.36.coup_ref
  2.1 24.1 %shard_map.138 = (bf16[4,8,64,256]{3,2,1,0:T(8,128)(2,1)}, f32[4,8,64,256]{3,2,1,0:T(8,128)}) custom-call(s32[128]{0:T(128)} %bitcast.43, s32[128]{0:T(128)} %reshape.36.coup_ref, bf16[32,512,512]{2,1,0:T(8,128)(2,1)} %upd_ref.1, bf16[64,16384]{1,0:T(8,128)(2,1)} %probe_ref.1, s32[32,4,128]{2,1,0:T(4,128)} %bitcast.42, bf16[64,128,128]{2,1,0:T(8,128)(2,1)} %blk_ref.1, ...), custom_call_target="tpu_custom_call" | custom-call | flops 20000000000 | bytes 16777216 | tf_op jit(solution)/shard_map/pallas_call | solution.py:118
  26.2 0.5 collective-permute-start
  26.6 2.5 %collective-permute-done = bf16[4,8,64,256]{3,2,1,0:T(8,128)(2,1)S(1)} collective-permute-done((bf16[4,8,64,256]{3,2,1,0:T(8,128)(2,1)}, bf16[4,8,64,256]{3,2,1,0:T(8,128)(2,1)S(1)}, u32[]{:S(2)}, u32[]{:S(2)}) %collective-permute-start) | collective-permute-done | bytes 1048608 | tf_op jit(solution)/shard_map/ppermute | solution.py:24
  29.1 1.9 %convert_add_fusion = f32[4,8,64,256]{3,2,1,0:T(8,128)S(1)} fusion(f32[4,8,64,256]{3,2,1,0:T(8,128)} %get-tuple-element.12, bf16[4,8,64,256]{3,2,1,0:T(8,128)(2,1)S(1)} %collective-permute-done), kind=kLoop, calls=%fused_computation | loop fusion | flops 1048576 | bytes 5242880 | tf_op jit(solution)/shard_map/add | solution.py:250
  31.0 0.0 copy-start.2
  31.0 0.2 fusion.7
  31.3 2.9 %collective-permute-start.3 = (bf16[2,4,64,256]{3,2,1,0:T(8,128)(2,1)S(1)}, bf16[2,4,64,256]{3,2,1,0:T(8,128)(2,1)S(1)}, u32[]{:S(2)}, u32[]{:S(2)}) collective-permute-start(bf16[2,4,64,256]{3,2,1,0:T(8,128)(2,1)S(1)} %fusion.1), channel_id=1, source_target_pairs={{0,16},{4,20},{8,24},{12,28},{16,0},{20,4},{24,8},{28,12},{1,17},{... | collective-permute-start | bytes 786440 | tf_op jit(solution)/shard_map/ppermute | solution.py:24
  34.2 0.0 copy-done.2
  34.2 1.6 %collective-permute-start.5 = (f32[64,128]{1,0:T(8,128)S(1)}, f32[64,128]{1,0:T(8,128)S(1)}, u32[]{:S(2)}, u32[]{:S(2)}) collective-permute-start(f32[64,128]{1,0:T(8,128)S(1)} %copy-done.2), channel_id=1, source_target_pairs={{0,1},{1,2},{2,3},{3,0},{4,5},{5,6},{6,7},{7,4},{8,9},{9,10},{10,1... | collective-permute-start | bytes 98312 | tf_op jit(solution)/shard_map/ppermute | solution.py:34
  35.8 2.6 %collective-permute-start.6 = (f32[64,128]{1,0:T(8,128)S(1)}, f32[64,128]{1,0:T(8,128)S(1)}, u32[]{:S(2)}, u32[]{:S(2)}) collective-permute-start(f32[64,128]{1,0:T(8,128)S(1)} %copy-done.2), channel_id=1, source_target_pairs={{0,2},{1,3},{2,0},{3,1},{4,6},{5,7},{6,4},{7,5},{8,10},{9,11},{10,... | collective-permute-start | bytes 98312 | tf_op jit(solution)/shard_map/ppermute | solution.py:34
  38.4 1.4 %collective-permute-start.7 = (f32[64,128]{1,0:T(8,128)S(1)}, f32[64,128]{1,0:T(8,128)S(1)}, u32[]{:S(2)}, u32[]{:S(2)}) collective-permute-start(f32[64,128]{1,0:T(8,128)S(1)} %copy-done.2), channel_id=1, source_target_pairs={{0,3},{1,0},{2,1},{3,2},{4,7},{5,4},{6,5},{7,6},{8,11},{9,8},{10,9... | collective-permute-start | bytes 98312 | tf_op jit(solution)/shard_map/ppermute | solution.py:34
  39.8 1.6 %collective-permute-start.1 = (bf16[2,4,64,256]{3,2,1,0:T(8,128)(2,1)S(1)}, bf16[2,4,64,256]{3,2,1,0:T(8,128)(2,1)S(1)}, u32[]{:S(2)}, u32[]{:S(2)}) collective-permute-start(bf16[2,4,64,256]{3,2,1,0:T(8,128)(2,1)S(1)} %fusion), channel_id=1, source_target_pairs={{0,8},{4,12},{8,0},{12,4},{16,24},{20,28},{24,16},{28,20},{1,9},{5... | collective-permute-start | bytes 786440 | tf_op jit(solution)/shard_map/ppermute | solution.py:24
  41.4 0.0 collective-permute-done.3
  41.4 0.1 bitcast_add_fusion
  41.5 1.3 %collective-permute-start.4 = (bf16[4,64,256]{2,1,0:T(8,128)(2,1)S(1)}, bf16[4,64,256]{2,1,0:T(8,128)(2,1)S(1)}, u32[]{:S(2)}, u32[]{:S(2)}) collective-permute-start(bf16[4,64,256]{2,1,0:T(8,128)(2,1)S(1)} %fusion.5), channel_id=1, source_target_pairs={{0,8},{4,12},{8,0},{12,4},{16,24},{20,28},{24,16},{28,20},{1,9},{5... | collective-permute-start | bytes 393224 | tf_op jit(solution)/shard_map/ppermute | solution.py:24
  42.7 5.8 %collective-permute-done.1 = bf16[2,4,64,256]{3,2,1,0:T(8,128)(2,1)S(1)} collective-permute-done((bf16[2,4,64,256]{3,2,1,0:T(8,128)(2,1)S(1)}, bf16[2,4,64,256]{3,2,1,0:T(8,128)(2,1)S(1)}, u32[]{:S(2)}, u32[]{:S(2)}) %collective-permute-start.1) | collective-permute-done | bytes 262176 | tf_op jit(solution)/shard_map/ppermute | solution.py:24
  48.5 0.1 bitcast_add_fusion.1
  48.6 0.8 collective-permute-start.2
  49.3 0.5 collective-permute-done.4
  49.9 3.7 %collective-permute-done.2 = bf16[4,64,256]{2,1,0:T(8,128)(2,1)S(1)} collective-permute-done((bf16[4,64,256]{2,1,0:T(8,128)(2,1)S(1)}, bf16[4,64,256]{2,1,0:T(8,128)(2,1)S(1)}, u32[]{:S(2)}, u32[]{:S(2)}) %collective-permute-start.2) | collective-permute-done | bytes 131104 | tf_op jit(solution)/shard_map/ppermute | solution.py:24
  53.6 0.7 pad_maximum_fusion
  54.4 3.6 %all-to-all-start = ((bf16[4,2,64,256]{3,2,1,0:T(8,128)(2,1)}), bf16[4,2,64,256]{3,2,1,0:T(8,128)(2,1)S(1)}, u32[]{:S(2)}, u32[]{:S(2)}) async-start(bf16[4,2,64,256]{3,2,1,0:T(8,128)(2,1)} %bitcast.11), calls=%async_computation | async-start | bytes 524288 | tf_op jit(solution)/shard_map/all_to_all | solution.py:260
  58.1 0.0 collective-permute-done.5
  58.1 0.0 collective-permute-done.6
  58.1 0.0 collective-permute-done.7
  58.1 6.5 %all-to-all-done = bf16[4,2,64,256]{3,2,1,0:T(8,128)(2,1)S(1)} async-done(((bf16[4,2,64,256]{3,2,1,0:T(8,128)(2,1)}), bf16[4,2,64,256]{3,2,1,0:T(8,128)(2,1)S(1)}, u32[]{:S(2)}, u32[]{:S(2)}) %all-to-all-start) | async-done | bytes 262176 | tf_op jit(solution)/shard_map/all_to_all | solution.py:260
  64.6 0.3 copy.20
  64.9 0.5 fusion.8.sketched_ref
  65.4 0.6 fusion.9
  66.0 2.6 %collective-permute-start.8 = (f32[128,128]{1,0:T(8,128)S(1)}, f32[128,128]{1,0:T(8,128)S(1)}, u32[]{:S(2)}, u32[]{:S(2)}) collective-permute-start(f32[128,128]{1,0:T(8,128)S(1)} %fusion.9), channel_id=1, source_target_pairs={{0,1},{1,0},{2,3},{3,2},{4,5},{5,4},{6,7},{7,6},{8,9},{9,8},{10,11... | collective-permute-start | bytes 196616 | tf_op jit(solution)/shard_map/ppermute | solution.py:24
  68.6 0.4 fusion.10
  69.0 0.1 collective-permute-start.10
  69.7 1.6 %collective-permute-done.8 = f32[128,128]{1,0:T(8,128)S(1)} collective-permute-done((f32[128,128]{1,0:T(8,128)S(1)}, f32[128,128]{1,0:T(8,128)S(1)}, u32[]{:S(2)}, u32[]{:S(2)}) %collective-permute-start.8) | collective-permute-done | bytes 65568 | tf_op jit(solution)/shard_map/ppermute | solution.py:24
  71.4 1.1 collective-permute-start.9
  72.5 1.8 %collective-permute-done.10 = f32[256,128]{1,0:T(8,128)S(1)} collective-permute-done((f32[256,128]{1,0:T(8,128)S(1)}, f32[256,128]{1,0:T(8,128)S(1)}, u32[]{:S(2)}, u32[]{:S(2)}) %collective-permute-start.10) | collective-permute-done | bytes 131104 | tf_op jit(solution)/shard_map/ppermute | solution.py:24
  74.3 0.2 collective-permute-start.11
  74.5 2.1 %collective-permute-done.9 = f32[128,128]{1,0:T(8,128)S(1)} collective-permute-done((f32[128,128]{1,0:T(8,128)S(1)}, f32[128,128]{1,0:T(8,128)S(1)}, u32[]{:S(2)}, u32[]{:S(2)}) %collective-permute-start.9) | collective-permute-done | bytes 65568 | tf_op jit(solution)/shard_map/ppermute | solution.py:24
  76.6 0.0 copy-start
  76.6 12.5 %shard_map.139 = (f32[512,128]{1,0:T(8,128)}, f32[128,128]{1,0:T(8,128)S(1)}) custom-call(s32[1]{0:T(128)} %copy.26.rank_ref, f32[128,128]{1,0:T(8,128)S(1)} %add.121.gram_ref, f32[512,128]{1,0:T(8,128)S(1)} %fusion.8.sketched_ref), custom_call_target="tpu_custom_call" | custom-call | flops 12000000000 | bytes 524288 | tf_op jit(solution)/shard_map/pallas_call | solution.py:203
  89.1 0.0 collective-permute-done.11
  89.1 0.3 convolution_select_fusion.own_ref
  89.4 0.0 copy-start.1
  89.4 0.1 collective-permute-start.12
  89.5 1.3 %collective-permute-done.12.partner_ref = f32[256,128]{1,0:T(8,128)S(1)} collective-permute-done((f32[256,128]{1,0:T(8,128)S(1)}, f32[256,128]{1,0:T(8,128)S(1)}, u32[]{:S(2)}, u32[]{:S(2)}) %collective-permute-start.12) | collective-permute-done | bytes 131104 | tf_op jit(solution)/shard_map/ppermute | solution.py:24
  90.9 0.0 copy-done
  90.9 13.9 %shard_map.140 = (f32[128,128]{1,0:T(8,128)}, f32[256,128]{1,0:T(8,128)S(1)}) custom-call(s32[4]{0:T(128)S(1)} %copy-done, f32[256,128]{1,0:T(8,128)S(1)} %convolution_select_fusion.own_ref, f32[256,128]{1,0:T(8,128)S(1)} %collective-permute-done.12.partner_ref, f32[256,128]{1,0:T(8,128)S(1)} %constant_dynamic-update-slice_fusion.sketch_ref), custom_call_target="tpu_custom_call" | custom-call | flops 12000000000 | bytes 524288 | tf_op jit(solution)/shard_map/pallas_call | solution.py:203
  104.8 1.5 %collective-permute-start.13 = (f32[256,128]{1,0:T(8,128)S(1)}, f32[256,128]{1,0:T(8,128)S(1)}, u32[]{:S(2)}, u32[]{:S(2)}) collective-permute-start(f32[256,128]{1,0:T(8,128)S(1)} %get-tuple-element.17.own_ref), channel_id=1, source_target_pairs={{0,8},{4,12},{8,0},{12,4},{16,24},{20,28},{24,16},{28,20},{1,9},{5... | collective-permute-start | bytes 393224 | tf_op jit(solution)/shard_map/ppermute | solution.py:24
  106.3 4.0 %collective-permute-done.13.partner_ref = f32[256,128]{1,0:T(8,128)S(1)} collective-permute-done((f32[256,128]{1,0:T(8,128)S(1)}, f32[256,128]{1,0:T(8,128)S(1)}, u32[]{:S(2)}, u32[]{:S(2)}) %collective-permute-start.13) | collective-permute-done | bytes 131104 | tf_op jit(solution)/shard_map/ppermute | solution.py:24
  110.3 0.0 copy-done.1
  110.3 13.9 %shard_map.141 = (f32[128,128]{1,0:T(8,128)}, f32[256,128]{1,0:T(8,128)S(1)}) custom-call(s32[2]{0:T(128)S(1)} %copy-done.1, f32[256,128]{1,0:T(8,128)S(1)} %get-tuple-element.17.own_ref, f32[256,128]{1,0:T(8,128)S(1)} %collective-permute-done.13.partner_ref, f32[256,128]{1,0:T(8,128)S(1)} %constant_dynamic-update-slice_fusion.sketch_ref), custom_call_target="tpu_custom_call" | custom-call | flops 12000000000 | bytes 524288 | tf_op jit(solution)/shard_map/pallas_call | solution.py:203
  124.2 0.6 constant_dynamic-slice_fusion
  (16 shorter events, 0.3 us)
Async XLA Ops:
  26.2 3.0 %collective-permute-start = (bf16[4,8,64,256]{3,2,1,0:T(8,128)(2,1)}, bf16[4,8,64,256]{3,2,1,0:T(8,128)(2,1)S(1)}, u32[]{:S(2)}, u32[]{:S(2)}) collective-permute-start(bf16[4,8,64,256]{3,2,1,0:T(8,128)(2,1)} %get-tuple-element.13), channel_id=1, source_target_pairs={{0,4},{4,0},{8,12},{12,8},{16,20},{20,16},{24,28},{28,24},{1,5},{5... | collective-permute-start | bytes 3145736 | tf_op jit(solution)/shard_map/ppermute | solution.py:24
  31.0 3.2 %copy-start.2 = (f32[64,128]{1,0:T(8,128)S(1)}, f32[64,128]{1,0:T(8,128)}, u32[]{:S(2)}) copy-start(f32[64,128]{1,0:T(8,128)} %param.18) | copy-start | bytes 98308
  31.3 10.1 %collective-permute-start.3 = (bf16[2,4,64,256]{3,2,1,0:T(8,128)(2,1)S(1)}, bf16[2,4,64,256]{3,2,1,0:T(8,128)(2,1)S(1)}, u32[]{:S(2)}, u32[]{:S(2)}) collective-permute-start(bf16[2,4,64,256]{3,2,1,0:T(8,128)(2,1)S(1)} %fusion.1), channel_id=1, source_target_pairs={{0,16},{4,20},{8,24},{12,28},{16,0},{20,4},{24,8},{28,12},{1,17},{... | collective-permute-start | bytes 786440 | tf_op jit(solution)/shard_map/ppermute | solution.py:24
  34.2 23.8 %collective-permute-start.5 = (f32[64,128]{1,0:T(8,128)S(1)}, f32[64,128]{1,0:T(8,128)S(1)}, u32[]{:S(2)}, u32[]{:S(2)}) collective-permute-start(f32[64,128]{1,0:T(8,128)S(1)} %copy-done.2), channel_id=1, source_target_pairs={{0,1},{1,2},{2,3},{3,0},{4,5},{5,6},{6,7},{7,4},{8,9},{9,10},{10,1... | collective-permute-start | bytes 98312 | tf_op jit(solution)/shard_map/ppermute | solution.py:34
  35.8 22.3 %collective-permute-start.6 = (f32[64,128]{1,0:T(8,128)S(1)}, f32[64,128]{1,0:T(8,128)S(1)}, u32[]{:S(2)}, u32[]{:S(2)}) collective-permute-start(f32[64,128]{1,0:T(8,128)S(1)} %copy-done.2), channel_id=1, source_target_pairs={{0,2},{1,3},{2,0},{3,1},{4,6},{5,7},{6,4},{7,5},{8,10},{9,11},{10,... | collective-permute-start | bytes 98312 | tf_op jit(solution)/shard_map/ppermute | solution.py:34
  38.4 19.7 %collective-permute-start.7 = (f32[64,128]{1,0:T(8,128)S(1)}, f32[64,128]{1,0:T(8,128)S(1)}, u32[]{:S(2)}, u32[]{:S(2)}) collective-permute-start(f32[64,128]{1,0:T(8,128)S(1)} %copy-done.2), channel_id=1, source_target_pairs={{0,3},{1,0},{2,1},{3,2},{4,7},{5,4},{6,5},{7,6},{8,11},{9,8},{10,9... | collective-permute-start | bytes 98312 | tf_op jit(solution)/shard_map/ppermute | solution.py:34
  39.8 8.7 %collective-permute-start.1 = (bf16[2,4,64,256]{3,2,1,0:T(8,128)(2,1)S(1)}, bf16[2,4,64,256]{3,2,1,0:T(8,128)(2,1)S(1)}, u32[]{:S(2)}, u32[]{:S(2)}) collective-permute-start(bf16[2,4,64,256]{3,2,1,0:T(8,128)(2,1)S(1)} %fusion), channel_id=1, source_target_pairs={{0,8},{4,12},{8,0},{12,4},{16,24},{20,28},{24,16},{28,20},{1,9},{5... | collective-permute-start | bytes 786440 | tf_op jit(solution)/shard_map/ppermute | solution.py:24
  41.5 8.4 %collective-permute-start.4 = (bf16[4,64,256]{2,1,0:T(8,128)(2,1)S(1)}, bf16[4,64,256]{2,1,0:T(8,128)(2,1)S(1)}, u32[]{:S(2)}, u32[]{:S(2)}) collective-permute-start(bf16[4,64,256]{2,1,0:T(8,128)(2,1)S(1)} %fusion.5), channel_id=1, source_target_pairs={{0,8},{4,12},{8,0},{12,4},{16,24},{20,28},{24,16},{28,20},{1,9},{5... | collective-permute-start | bytes 393224 | tf_op jit(solution)/shard_map/ppermute | solution.py:24
  48.6 5.0 %collective-permute-start.2 = (bf16[4,64,256]{2,1,0:T(8,128)(2,1)S(1)}, bf16[4,64,256]{2,1,0:T(8,128)(2,1)S(1)}, u32[]{:S(2)}, u32[]{:S(2)}) collective-permute-start(bf16[4,64,256]{2,1,0:T(8,128)(2,1)S(1)} %fusion.4), channel_id=1, source_target_pairs={{0,16},{4,20},{8,24},{12,28},{16,0},{20,4},{24,8},{28,12},{1,17},{... | collective-permute-start | bytes 393224 | tf_op jit(solution)/shard_map/ppermute | solution.py:24
  54.4 10.3 %all-to-all-start = ((bf16[4,2,64,256]{3,2,1,0:T(8,128)(2,1)}), bf16[4,2,64,256]{3,2,1,0:T(8,128)(2,1)S(1)}, u32[]{:S(2)}, u32[]{:S(2)}) async-start(bf16[4,2,64,256]{3,2,1,0:T(8,128)(2,1)} %bitcast.11), calls=%async_computation | async-start | bytes 524288 | tf_op jit(solution)/shard_map/all_to_all | solution.py:260
  66.0 5.3 %collective-permute-start.8 = (f32[128,128]{1,0:T(8,128)S(1)}, f32[128,128]{1,0:T(8,128)S(1)}, u32[]{:S(2)}, u32[]{:S(2)}) collective-permute-start(f32[128,128]{1,0:T(8,128)S(1)} %fusion.9), channel_id=1, source_target_pairs={{0,1},{1,0},{2,3},{3,2},{4,5},{5,4},{6,7},{7,6},{8,9},{9,8},{10,11... | collective-permute-start | bytes 196616 | tf_op jit(solution)/shard_map/ppermute | solution.py:24
  69.0 5.2 %collective-permute-start.10 = (f32[256,128]{1,0:T(8,128)S(1)}, f32[256,128]{1,0:T(8,128)S(1)}, u32[]{:S(2)}, u32[]{:S(2)}) collective-permute-start(f32[256,128]{1,0:T(8,128)S(1)} %fusion.10), channel_id=1, source_target_pairs={{0,1},{1,0},{2,3},{3,2},{4,5},{5,4},{6,7},{7,6},{8,9},{9,8},{10,11... | collective-permute-start | bytes 393224 | tf_op jit(solution)/shard_map/ppermute | solution.py:24
  71.4 5.2 %collective-permute-start.9 = (f32[128,128]{1,0:T(8,128)S(1)}, f32[128,128]{1,0:T(8,128)S(1)}, u32[]{:S(2)}, u32[]{:S(2)}) collective-permute-start(f32[128,128]{1,0:T(8,128)S(1)} %add.120), channel_id=1, source_target_pairs={{0,2},{1,3},{2,0},{3,1},{4,6},{5,7},{6,4},{7,5},{8,10},{9,11},{10,... | collective-permute-start | bytes 196616 | tf_op jit(solution)/shard_map/ppermute | solution.py:24
  74.3 14.9 %collective-permute-start.11 = (f32[256,128]{1,0:T(8,128)S(1)}, f32[256,128]{1,0:T(8,128)S(1)}, u32[]{:S(2)}, u32[]{:S(2)}) collective-permute-start(f32[256,128]{1,0:T(8,128)S(1)} %add.122), channel_id=1, source_target_pairs={{0,2},{1,3},{2,0},{3,1},{4,6},{5,7},{6,4},{7,5},{8,10},{9,11},{10,... | collective-permute-start | bytes 393224 | tf_op jit(solution)/shard_map/ppermute | solution.py:24
  76.6 14.2 %copy-start = (s32[4]{0:T(128)S(1)}, s32[4]{0:T(128)}, u32[]{:S(2)}) copy-start(s32[4]{0:T(128)} %rank_ref.3) | copy-start | bytes 52
  89.4 20.9 %copy-start.1 = (s32[2]{0:T(128)S(1)}, s32[2]{0:T(128)}, u32[]{:S(2)}) copy-start(s32[2]{0:T(128)} %rank_ref.4) | copy-start | bytes 28
  89.4 1.4 %collective-permute-start.12 = (f32[256,128]{1,0:T(8,128)S(1)}, f32[256,128]{1,0:T(8,128)S(1)}, u32[]{:S(2)}, u32[]{:S(2)}) collective-permute-start(f32[256,128]{1,0:T(8,128)S(1)} %convolution_select_fusion.own_ref), channel_id=1, source_target_pairs={{0,4},{4,0},{8,12},{12,8},{16,20},{20,16},{24,28},{28,24},{1,5},{5... | collective-permute-start | bytes 393224 | tf_op jit(solution)/shard_map/ppermute | solution.py:24
  104.8 5.5 %collective-permute-start.13 = (f32[256,128]{1,0:T(8,128)S(1)}, f32[256,128]{1,0:T(8,128)S(1)}, u32[]{:S(2)}, u32[]{:S(2)}) collective-permute-start(f32[256,128]{1,0:T(8,128)S(1)} %get-tuple-element.17.own_ref), channel_id=1, source_target_pairs={{0,8},{4,12},{8,0},{12,4},{16,24},{20,28},{24,16},{28,20},{1,9},{5... | collective-permute-start | bytes 393224 | tf_op jit(solution)/shard_map/ppermute | solution.py:24
